TPU v7x, 32 devices: a whole 2x2x4 slice. The times are simulated.
32 devices in a mesh: groups: 2 (over y), outer: 4 (over z), bulk: 2 (over x), inner: 2 (over core).
Axes of the slice: x: 2, y: 2, z: 4, core: 2. Of those that a mesh axis runs over, the one named last changes fastest.
Arguments:
- points: bfloat16 [2048, 1152], P(('groups', 'outer', 'bulk', 'inner')), parts along dimension 0, may hold values from -17 to 17
- coarse_ids: int32 [2048, 8], P(('groups', 'outer', 'bulk', 'inner')), parts along dimension 0, may hold values from 0 to 511, as said below
- fine_cent: bfloat16 [1024, 128, 1152], P(('groups', 'outer', 'bulk', 'inner')), parts along dimension 0, may hold values from -6 to 6
- slot_live: int32 [1024, 128], P(('groups', 'outer', 'bulk', 'inner')), parts along dimension 0, may hold values from 0 to 1, as said below
- coarse_cent: bfloat16 [1024, 1152], P(('groups', 'outer', 'bulk', 'inner')), parts along dimension 0, may hold values from -6 to 6
Outputs:
- fine_out: bfloat16 [1024, 128, 1152], P(('groups', 'outer', 'bulk', 'inner')), parts along dimension 0
- coarse_out: bfloat16 [1024, 1152], P(('groups', 'outer', 'bulk', 'inner')), parts along dimension 0
There are 2 independent parts, one for each index of `groups`. A program takes and returns all parts, laid end to end along the dimension named above; each array names one. Nothing has to cross between parts.
Inputs may be any that keep to these rules, and one draw needn't show every extreme that they name: `coarse_ids`: each row names 8 different coarse clusters. Within the rows of one device no coarse cluster is named by more than 2 rows, and on every device some clusters are named by exactly 2 rows. `slot_live`: slots 0 and 1 of every block are live.
All inputs are finite; a program needn't handle non-finite values.
Results may differ from a plain program's by a relative error of at most 0.0055.
Values may be sent and summed in bfloat16 or wider, within the bound.
A program may use at most 128 MiB of HBM per device.

v0:
```python
import math

import jax
import jax.numpy as jnp
from jax import lax
from jax.sharding import PartitionSpec as P

MOST = 2
ITERS = 2


PRIOR = 1.0


def shards(points, coarse_ids, fine_cent, slot_live, coarse_cent):
    point_rows, top_count = coarse_ids.shape
    block_count, slot_width, feature = fine_cent.shape
    outer_size = lax.axis_size("outer")
    group_size = lax.axis_size(("bulk", "inner"))
    owner_count = outer_size * group_size
    slot_total = block_count * owner_count * MOST
    pair_total = point_rows * top_count
    pair_ids = coarse_ids.reshape(pair_total)
    positions = jnp.arange(pair_total, dtype=jnp.int32)
    same_cluster = (pair_ids[:, None] == pair_ids[None, :]) & (
        positions[None, :] < positions[:, None]
    )
    pair_rank = jnp.sum(same_cluster.astype(jnp.int32), axis=1)
    slot_index = pair_ids * MOST + pair_rank
    slot_source = jnp.full((slot_total,), pair_total, jnp.int32).at[slot_index].set(positions)
    occupied = slot_source < pair_total
    source_point = jnp.minimum(slot_source, pair_total - 1) // top_count
    outgoing = jnp.where(occupied[:, None], points[source_point], jnp.zeros((), jnp.bfloat16))
    outgoing = outgoing.reshape(outer_size, group_size, block_count * MOST, feature)
    received = lax.all_to_all(
        lax.all_to_all(outgoing, "outer", split_axis=0, concat_axis=0, tiled=True),
        ("bulk", "inner"),
        split_axis=1,
        concat_axis=1,
        tiled=True,
    )
    received = received.reshape(owner_count, block_count, MOST, feature)
    live_mask = slot_live == 1
    inv_root = 1.0 / math.sqrt(feature)
    point_of_pair = positions // top_count
    fine_now = fine_cent
    coarse_now = coarse_cent
    for step_index in range(ITERS):
        fine_wide = fine_now.astype(jnp.float32)
        half_fine = 0.5 * jnp.sum(fine_wide * fine_wide, axis=-1)
        products = jnp.einsum(
            "nbmd,bsd->nbms", received, fine_now, preferred_element_type=jnp.float32
        )
        logits = (products - half_fine[None, :, None, :]) * inv_root
        masked = jnp.where(live_mask[None, :, None, :], logits, -jnp.inf)
        slot_max = jnp.max(masked, axis=-1)
        slot_sum = jnp.sum(jnp.exp(masked - slot_max[..., None]), axis=-1)
        back_max, back_sum = (
            lax.all_to_all(
                lax.all_to_all(
                    slot_max.reshape(outer_size, group_size, block_count * MOST),
                    "outer",
                    split_axis=0,
                    concat_axis=0,
                    tiled=True,
                ),
                ("bulk", "inner"),
                split_axis=1,
                concat_axis=1,
                tiled=True,
            ),
            lax.all_to_all(
                lax.all_to_all(
                    slot_sum.reshape(outer_size, group_size, block_count * MOST),
                    "outer",
                    split_axis=0,
                    concat_axis=0,
                    tiled=True,
                ),
                ("bulk", "inner"),
                split_axis=1,
                concat_axis=1,
                tiled=True,
            ),
        )
        pair_max = back_max.reshape(slot_total)[slot_index]
        pair_sum = back_sum.reshape(slot_total)[slot_index]
        all_coarse = lax.all_gather(coarse_now, ("outer", "bulk", "inner"), axis=0, tiled=True)
        all_wide = all_coarse.astype(jnp.float32)
        half_all = 0.5 * jnp.sum(all_wide * all_wide, axis=-1)
        picked = all_coarse[pair_ids].reshape(point_rows, top_count, feature)
        coarse_dot = jnp.einsum("pd,pkd->pk", points, picked, preferred_element_type=jnp.float32)
        coarse_shift = (coarse_dot.reshape(pair_total) - half_all[pair_ids]) * inv_root
        grid_max = (pair_max + coarse_shift).reshape(point_rows, top_count)
        point_max = jnp.max(grid_max, axis=1)
        point_sum = jnp.sum(
            pair_sum.reshape(point_rows, top_count) * jnp.exp(grid_max - point_max[:, None]), axis=1
        )
        point_inv = 1.0 / point_sum
        pair_shift = point_max[point_of_pair] - coarse_shift
        pair_inv = point_inv[point_of_pair]
        shift_slots = jnp.zeros((slot_total,), jnp.float32).at[slot_index].set(pair_shift)
        inv_slots = jnp.zeros((slot_total,), jnp.float32).at[slot_index].set(pair_inv)
        got_shift, got_inv = (
            lax.all_to_all(
                lax.all_to_all(
                    shift_slots.reshape(outer_size, group_size, block_count * MOST),
                    "outer",
                    split_axis=0,
                    concat_axis=0,
                    tiled=True,
                ),
                ("bulk", "inner"),
                split_axis=1,
                concat_axis=1,
                tiled=True,
            ),
            lax.all_to_all(
                lax.all_to_all(
                    inv_slots.reshape(outer_size, group_size, block_count * MOST),
                    "outer",
                    split_axis=0,
                    concat_axis=0,
                    tiled=True,
                ),
                ("bulk", "inner"),
                split_axis=1,
                concat_axis=1,
                tiled=True,
            ),
        )
        got_shift = got_shift.reshape(owner_count, block_count, MOST)
        got_inv = got_inv.reshape(owner_count, block_count, MOST)
        weights = (jnp.exp(masked - got_shift[..., None]) * got_inv[..., None]).astype(jnp.bfloat16)
        mass = PRIOR + jnp.sum(weights.astype(jnp.float32), axis=(0, 2))
        totals = PRIOR * fine_wide + jnp.einsum(
            "nbms,nbmd->bsd", weights, received, preferred_element_type=jnp.float32
        )
        fine_now = jnp.where(live_mask[..., None], totals / mass[..., None], fine_wide).astype(
            jnp.bfloat16
        )
        live_mass = jnp.where(live_mask, mass, 0.0)
        coarse_now = (
            jnp.einsum(
                "bs,bsd->bd",
                live_mass,
                fine_now.astype(jnp.float32),
                precision=lax.Precision.HIGHEST,
            )
            / jnp.sum(live_mass, axis=1)[:, None]
        ).astype(jnp.bfloat16)
    return (fine_now, coarse_now)


def solution(mesh):
    in_specs = (
        P(("groups", "outer", "bulk", "inner"), None),
        P(("groups", "outer", "bulk", "inner"), None),
        P(("groups", "outer", "bulk", "inner"), None, None),
        P(("groups", "outer", "bulk", "inner"), None),
        P(("groups", "outer", "bulk", "inner"), None),
    )
    out_specs = (
        P(("groups", "outer", "bulk", "inner"), None, None),
        P(("groups", "outer", "bulk", "inner"), None),
    )
    return jax.shard_map(shards, mesh=mesh, in_specs=in_specs, out_specs=out_specs, check_vma=False)
```

profile of v0, /device:TPU:0, one launch (start us, length us, event | category | flops | bytes accessed | tf_op | source)
XLA Modules:
  0.0 505.4 jit_solution(10722261909556460996)
XLA Ops:
  11.2 4.2 gather_fusion
  18.3 6.3 %all-to-all-start = ((bf16[4,4,64,1152]{3,1,2,0:T(4,128)(2,1)}), bf16[4,4,64,1152]{3,1,2,0:T(4,128)(2,1)S(1)}, u32[]{:S(2)}, u32[]{:S(2)}) async-start(bf16[4,4,64,1152]{3,1,2,0:T(4,128)(2,1)} %copy_select_fusion), calls=%async_computation | async-start | bytes 4718592 | tf_op jit(solution)/shard_map/all_to_all | solution.py:36
  25.3 57.9 %all-to-all-done = bf16[4,4,64,1152]{3,1,2,0:T(4,128)(2,1)S(1)} async-done(((bf16[4,4,64,1152]{3,1,2,0:T(4,128)(2,1)}), bf16[4,4,64,1152]{3,1,2,0:T(4,128)(2,1)S(1)}, u32[]{:S(2)}, u32[]{:S(2)}) %all-to-all-start) | async-done | bytes 2359328 | tf_op jit(solution)/shard_map/all_to_all | solution.py:36
  83.3 3.2 copy.60
  86.5 3.9 all-to-all-start.1
  92.4 5.6 %fusion = f32[32,128]{1,0:T(8,128)S(1)} fusion(bf16[32,128,1152]{2,1,0:T(8,128)(2,1)} %param.7), kind=kLoop, calls=%fused_computation.20 | loop fusion | flops 14151680 | bytes 9453568 | tf_op jit(solution)/shard_map/reduce_sum | solution.py:50
  98.1 5.1 %gather_fusion.2 = bf16[512,1152]{1,0:T(8,128)(2,1)} fusion(bf16[512,1152]{1,0:T(8,128)(2,1)} %all-gather.3.cloned.1.call-done, s32[1024]{0:T(1024)S(1)} %pad_clamp_fusion), kind=kCustom, calls=%fused_computation.2 | custom fusion | bytes 2361344 | tf_op jit(solution)/shard_map/gather | solution.py:91
  105.4 13.5 %all-to-all-done.1 = bf16[4,4,64,1152]{3,0,2,1:T(4,128)(2,1)S(1)} async-done(((bf16[4,4,64,1152]{3,0,2,1:T(4,128)(2,1)}), bf16[4,4,64,1152]{3,0,2,1:T(4,128)(2,1)S(1)}, u32[]{:S(2)}, u32[]{:S(2)}) %all-to-all-start.1) | async-done | bytes 2359328 | tf_op jit(solution)/shard_map/all_to_all | solution.py:35
  118.9 4.4 copy.61
  123.3 5.0 reshape.202
  128.3 7.9 %fusion.77 = (f32[16,32,2]{0,2,1:T(2,128)S(1)}, f32[16,32,2,128]{3,0,2,1:T(8,128)S(1)}) fusion(f32[32,128]{1,0:T(8,128)S(1)} %broadcast_multiply_fusion.1, bf16[16,32,2,1152]{3,0,2,1:T(8,128)(2,1)} %reshape.202, bf16[32,128,1152]{2,1,0:T(8,128)(2,1)} %param.7, pred[32,128]{1,0:T(8,128)(4,1)S(1)} %broadcast_compare_fusion), kind=kOutput, calls=%fused_computation.195 | convolution fusion | flops 302513152 | bytes 12345344 | tf_op jit(solution)/shard_map/nbmd,bsd->nbms/dot_general | solution.py:51
  137.2 3.2 all-to-all-start.2
  141.8 4.2 all-to-all-done.2
  146.0 3.2 all-to-all-start.6
  151.4 3.4 all-to-all-done.6
  154.8 3.5 all-to-all-start.3
  158.2 3.5 gather_fusion.3
  163.3 3.3 all-to-all-start.7
  178.9 4.4 select_select_fusion.3
  183.3 35.7 %select_subtract_fusion.1 = f32[512]{0:T(512)S(1)} fusion(pred[512]{0:T(512)(128)(4,1)S(1)} %compare_reduce_fusion, pred[512]{0:T(512)(128)(4,1)S(1)} %compare_reduce_fusion.1, pred[512]{0:T(512)(128)(4,1)S(1)} %compare_reduce_fusion.2, pred[512]{0:T(512)(128)(4,1)S(1)} %compare_reduce_fusion.3, pred[512]{0:T(512)(128)(4,1)S(1)} %compare_reduce_fusion.4, ...), kind=kLoop, calls=%fused_computation.153 | loop fusion | flops 30720 | bytes 37604 | tf_op jit(solution)/shard_map/sub | solution.py:100
  222.2 3.2 all-to-all-start.4
  225.5 4.3 select_select_fusion.2
  229.8 35.3 %select_select_fusion.5 = f32[512]{0:T(512)S(1)} fusion(pred[512]{0:T(512)(128)(4,1)S(1)} %compare_reduce_fusion, pred[512]{0:T(512)(128)(4,1)S(1)} %compare_reduce_fusion.1, pred[512]{0:T(512)(128)(4,1)S(1)} %compare_reduce_fusion.2, pred[512]{0:T(512)(128)(4,1)S(1)} %compare_reduce_fusion.3, pred[512]{0:T(512)(128)(4,1)S(1)} %compare_reduce_fusion.4, ...), kind=kLoop, calls=%fused_computation.152 | loop fusion | flops 29184 | bytes 33508 | tf_op jit(solution)/shard_map/gather | solution.py:101
  268.3 5.1 %all-to-all-start.8 = ((f32[4,1,256]{2,1,0:T(1,128)}), f32[4,1,256]{2,1,0:T(1,128)S(1)}, u32[]{:S(2)}, u32[]{:S(2)}) async-start(f32[4,1,256]{2,1,0:T(1,128)} %reshape.884), calls=%async_computation.8 | async-start | bytes 8192 | tf_op jit(solution)/shard_map/all_to_all | solution.py:119
  274.7 4.2 all-to-all-done.8
  279.0 3.3 all-to-all-start.5
  286.0 3.2 all-to-all-start.9
  294.7 9.3 %fusion.3 = (f32[32,128]{1,0:T(8,128)S(1)}, bf16[32,128,1152]{2,1,0:T(8,128)(2,1)S(1)}) fusion(f32[32,128]{1,0:T(8,128)S(1)} %get-tuple-element.7, bf16[16,32,2,1152]{3,0,2,1:T(8,128)(2,1)S(1)} %copy-done.5, f32[16,32,2,128]{3,0,2,1:T(8,128)S(1)} %get-tuple-element.267, f32[16,32,2]{0,2,1:T(2,128)S(1)} %mul.101, f32[16,32,2]{0,2,1:T(2,128)S(1)} %sub.113, ...), kind=kOutput, calls=%fused_computation.23 | convolution fusion | flops 340127744 | bytes 21803008 | tf_op jit(solution)/shard_map/nbms,nbmd->bsd/dot_general | solution.py:136
  304.1 4.2 fusion.79
  309.0 6.0 %fusion.78 = (f32[16,32,2]{0,2,1:T(2,128)S(1)}, f32[16,32,2,128]{3,0,2,1:T(8,128)S(1)}) fusion(f32[32,128]{1,0:T(8,128)S(1)} %broadcast_multiply_fusion, bf16[16,32,2,1152]{3,0,2,1:T(8,128)(2,1)S(1)} %copy-done.5, bf16[32,128,1152]{2,1,0:T(8,128)(2,1)} %copy-done.3, pred[32,128]{1,0:T(8,128)(4,1)S(1)} %broadcast_compare_fusion), kind=kOutput, calls=%fused_computation.196 | convolution fusion | flops 302513152 | bytes 12345344 | tf_op jit(solution)/shard_map/nbmd,bsd->nbms/dot_general | solution.py:51
  320.6 4.2 all-to-all-done.10
  324.8 3.2 all-to-all-start.14
  329.3 4.2 all-to-all-done.14
  333.5 3.2 all-to-all-start.11
  340.5 3.6 all-to-all-start.15
  351.1 5.1 %gather_fusion.6 = bf16[512,1152]{1,0:T(8,128)(2,1)} fusion(bf16[512,1152]{1,0:T(8,128)(2,1)} %all-gather.5.cloned.1.call-done, s32[1024]{0:T(1024)S(1)} %pad_clamp_fusion), kind=kCustom, calls=%fused_computation.6 | custom fusion | bytes 2361344 | tf_op jit(solution)/shard_map/gather | solution.py:91
  358.8 3.5 gather_fusion.7
  368.5 4.4 select_select_fusion.1
  372.9 35.8 %select_subtract_fusion = f32[512]{0:T(512)S(1)} fusion(pred[512]{0:T(512)(128)(4,1)S(1)} %compare_reduce_fusion, pred[512]{0:T(512)(128)(4,1)S(1)} %compare_reduce_fusion.1, pred[512]{0:T(512)(128)(4,1)S(1)} %compare_reduce_fusion.2, pred[512]{0:T(512)(128)(4,1)S(1)} %compare_reduce_fusion.3, pred[512]{0:T(512)(128)(4,1)S(1)} %compare_reduce_fusion.4, ...), kind=kLoop, calls=%fused_computation.151 | loop fusion | flops 30720 | bytes 37604 | tf_op jit(solution)/shard_map/sub | solution.py:100
  411.9 3.2 all-to-all-start.12
  415.1 4.4 select_select_fusion
  419.5 35.5 %select_select_fusion.4 = f32[512]{0:T(512)S(1)} fusion(pred[512]{0:T(512)(128)(4,1)S(1)} %compare_reduce_fusion, pred[512]{0:T(512)(128)(4,1)S(1)} %compare_reduce_fusion.1, pred[512]{0:T(512)(128)(4,1)S(1)} %compare_reduce_fusion.2, pred[512]{0:T(512)(128)(4,1)S(1)} %compare_reduce_fusion.3, pred[512]{0:T(512)(128)(4,1)S(1)} %compare_reduce_fusion.4, ...), kind=kLoop, calls=%fused_computation.150 | loop fusion | flops 29184 | bytes 33508 | tf_op jit(solution)/shard_map/gather | solution.py:101
  458.2 5.1 %all-to-all-start.16 = ((f32[4,1,256]{2,1,0:T(1,128)}), f32[4,1,256]{2,1,0:T(1,128)S(1)}, u32[]{:S(2)}, u32[]{:S(2)}) async-start(f32[4,1,256]{2,1,0:T(1,128)} %reshape.900), calls=%async_computation.16 | async-start | bytes 8192 | tf_op jit(solution)/shard_map/all_to_all | solution.py:119
  464.7 4.2 all-to-all-done.16
  468.9 3.2 all-to-all-start.13
  475.9 3.4 all-to-all-start.17
  484.7 8.7 %fusion.5 = bf16[32,128,1152]{2,1,0:T(8,128)(2,1)S(1)} fusion(bf16[32,128,1152]{2,1,0:T(8,128)(2,1)} %copy-done.3, bf16[16,32,2,1152]{3,0,2,1:T(8,128)(2,1)S(1)} %copy-done.5, f32[32,128]{1,0:T(8,128)S(1)} %get-tuple-element.6, pred[32,128]{1,0:T(8,128)(4,1)S(1)} %broadcast_compare_fusion, f32[16,32,2,128]{3,0,2,1:T(8,128)S(1)} %get-tuple-element.271, ...), kind=kOutput, calls=%fused_computation.25 | convolution fusion | flops 325976064 | bytes 21786624 | tf_op jit(solution)/shard_map/nbms,nbmd->bsd/dot_general | solution.py:136
  493.4 4.2 fusion.80
  (242 shorter events, 91.6 us)
Async XLA Ops:
  7.2 4.0 copy-start
  18.3 65.0 %all-to-all-start = ((bf16[4,4,64,1152]{3,1,2,0:T(4,128)(2,1)}), bf16[4,4,64,1152]{3,1,2,0:T(4,128)(2,1)S(1)}, u32[]{:S(2)}, u32[]{:S(2)}) async-start(bf16[4,4,64,1152]{3,1,2,0:T(4,128)(2,1)} %copy_select_fusion), calls=%async_computation | async-start | bytes 4718592 | tf_op jit(solution)/shard_map/all_to_all | solution.py:36
  24.6 73.5 %all-gather.3.cloned.1.call-start = ((), (), s32[]{:S(2)}) async-start(), calls=%async_computation.18 | async-start | bytes 1253376 | tf_op jit(solution)/shard_map/all_gather | solution.py:88
  86.5 5.9 %copy-start.6 = (s32[32,128]{1,0:T(8,128)S(1)}, s32[32,128]{1,0:T(8,128)}, u32[]{:S(2)}) copy-start(s32[32,128]{1,0:T(8,128)} %param.8) | copy-start | bytes 49156
  86.5 32.4 %all-to-all-start.1 = ((bf16[4,4,64,1152]{3,0,2,1:T(4,128)(2,1)}), bf16[4,4,64,1152]{3,0,2,1:T(4,128)(2,1)S(1)}, u32[]{:S(2)}, u32[]{:S(2)}) async-start(bf16[4,4,64,1152]{3,0,2,1:T(4,128)(2,1)} %copy.60), calls=%async_computation.1 | async-start | bytes 4718592 | tf_op jit(solution)/shard_map/all_to_all | solution.py:35
  128.3 20.9 %copy-start.1 = (bf16[512,1152]{1,0:T(8,128)(2,1)S(1)}, bf16[512,1152]{1,0:T(8,128)(2,1)}, u32[]{:S(2)}) copy-start(bf16[512,1152]{1,0:T(8,128)(2,1)} %all-gather.3.cloned.1.call-done) | copy-start | bytes 3538948
  137.2 8.8 %all-to-all-start.2 = ((f32[4,1,256]{2,1,0:T(1,128)}), f32[4,1,256]{2,1,0:T(1,128)S(1)}, u32[]{:S(2)}, u32[]{:S(2)}) async-start(f32[4,1,256]{2,1,0:T(1,128)} %reshape.880), calls=%async_computation.2 | async-start | bytes 8192 | tf_op jit(solution)/shard_map/all_to_all | solution.py:60
  146.0 8.8 %all-to-all-start.6 = ((f32[4,1,256]{2,1,0:T(1,128)}), f32[4,1,256]{2,1,0:T(1,128)S(1)}, u32[]{:S(2)}, u32[]{:S(2)}) async-start(f32[4,1,256]{2,1,0:T(1,128)} %reshape.876), calls=%async_computation.6 | async-start | bytes 8192 | tf_op jit(solution)/shard_map/all_to_all | solution.py:73
  154.8 8.5 %all-to-all-start.3 = ((f32[4,1,256]{2,1,0:T(1,128)}), f32[4,1,256]{2,1,0:T(1,128)S(1)}, u32[]{:S(2)}, u32[]{:S(2)}) async-start(f32[4,1,256]{2,1,0:T(1,128)} %reshape.882), calls=%async_computation.3 | async-start | bytes 8192 | tf_op jit(solution)/shard_map/all_to_all | solution.py:59
  163.3 9.4 %all-to-all-start.7 = ((f32[4,1,256]{2,1,0:T(1,128)}), f32[4,1,256]{2,1,0:T(1,128)S(1)}, u32[]{:S(2)}, u32[]{:S(2)}) async-start(f32[4,1,256]{2,1,0:T(1,128)} %reshape.878), calls=%async_computation.7 | async-start | bytes 8192 | tf_op jit(solution)/shard_map/all_to_all | solution.py:72
  169.7 125.1 %copy-start.5 = (bf16[16,32,2,1152]{3,0,2,1:T(8,128)(2,1)S(1)}, bf16[16,32,2,1152]{3,0,2,1:T(8,128)(2,1)}, u32[]{:S(2)}) copy-start(bf16[16,32,2,1152]{3,0,2,1:T(8,128)(2,1)} %reshape.202) | copy-start | bytes 7077892
  222.2 46.1 %all-to-all-start.4 = ((f32[4,1,256]{2,1,0:T(1,128)}), f32[4,1,256]{2,1,0:T(1,128)S(1)}, u32[]{:S(2)}, u32[]{:S(2)}) async-start(f32[4,1,256]{2,1,0:T(1,128)} %reshape.888), calls=%async_computation.4 | async-start | bytes 8192 | tf_op jit(solution)/shard_map/all_to_all | solution.py:106
  268.3 10.6 %all-to-all-start.8 = ((f32[4,1,256]{2,1,0:T(1,128)}), f32[4,1,256]{2,1,0:T(1,128)S(1)}, u32[]{:S(2)}, u32[]{:S(2)}) async-start(f32[4,1,256]{2,1,0:T(1,128)} %reshape.884), calls=%async_computation.8 | async-start | bytes 8192 | tf_op jit(solution)/shard_map/all_to_all | solution.py:119
  279.0 7.1 %all-to-all-start.5 = ((f32[4,1,256]{2,1,0:T(1,128)}), f32[4,1,256]{2,1,0:T(1,128)S(1)}, u32[]{:S(2)}, u32[]{:S(2)}) async-start(f32[4,1,256]{2,1,0:T(1,128)} %reshape.890), calls=%async_computation.5 | async-start | bytes 8192 | tf_op jit(solution)/shard_map/all_to_all | solution.py:105
  286.0 7.0 %all-to-all-start.9 = ((f32[4,1,256]{2,1,0:T(1,128)}), f32[4,1,256]{2,1,0:T(1,128)S(1)}, u32[]{:S(2)}, u32[]{:S(2)}) async-start(f32[4,1,256]{2,1,0:T(1,128)} %reshape.886), calls=%async_computation.9 | async-start | bytes 8192 | tf_op jit(solution)/shard_map/all_to_all | solution.py:118
  289.3 61.8 %all-gather.5.cloned.1.call-start = ((), (), s32[]{:S(2)}) async-start(), calls=%async_computation.19 | async-start | bytes 1253376 | tf_op jit(solution)/shard_map/all_gather | solution.py:88
  304.1 4.2 copy-start.3
  316.0 8.8 %all-to-all-start.10 = ((f32[4,1,256]{2,1,0:T(1,128)}), f32[4,1,256]{2,1,0:T(1,128)S(1)}, u32[]{:S(2)}, u32[]{:S(2)}) async-start(f32[4,1,256]{2,1,0:T(1,128)} %reshape.896), calls=%async_computation.10 | async-start | bytes 8192 | tf_op jit(solution)/shard_map/all_to_all | solution.py:60
  324.8 8.8 %all-to-all-start.14 = ((f32[4,1,256]{2,1,0:T(1,128)}), f32[4,1,256]{2,1,0:T(1,128)S(1)}, u32[]{:S(2)}, u32[]{:S(2)}) async-start(f32[4,1,256]{2,1,0:T(1,128)} %reshape.892), calls=%async_computation.14 | async-start | bytes 8192 | tf_op jit(solution)/shard_map/all_to_all | solution.py:73
  333.5 7.0 %all-to-all-start.11 = ((f32[4,1,256]{2,1,0:T(1,128)}), f32[4,1,256]{2,1,0:T(1,128)S(1)}, u32[]{:S(2)}, u32[]{:S(2)}) async-start(f32[4,1,256]{2,1,0:T(1,128)} %reshape.898), calls=%async_computation.11 | async-start | bytes 8192 | tf_op jit(solution)/shard_map/all_to_all | solution.py:59
  340.5 7.4 %all-to-all-start.15 = ((f32[4,1,256]{2,1,0:T(1,128)}), f32[4,1,256]{2,1,0:T(1,128)S(1)}, u32[]{:S(2)}, u32[]{:S(2)}) async-start(f32[4,1,256]{2,1,0:T(1,128)} %reshape.894), calls=%async_computation.15 | async-start | bytes 8192 | tf_op jit(solution)/shard_map/all_to_all | solution.py:72
  356.2 2.3 copy-start.2
  411.9 46.4 %all-to-all-start.12 = ((f32[4,1,256]{2,1,0:T(1,128)}), f32[4,1,256]{2,1,0:T(1,128)S(1)}, u32[]{:S(2)}, u32[]{:S(2)}) async-start(f32[4,1,256]{2,1,0:T(1,128)} %reshape.904), calls=%async_computation.12 | async-start | bytes 8192 | tf_op jit(solution)/shard_map/all_to_all | solution.py:106
  458.2 10.6 %all-to-all-start.16 = ((f32[4,1,256]{2,1,0:T(1,128)}), f32[4,1,256]{2,1,0:T(1,128)S(1)}, u32[]{:S(2)}, u32[]{:S(2)}) async-start(f32[4,1,256]{2,1,0:T(1,128)} %reshape.900), calls=%async_computation.16 | async-start | bytes 8192 | tf_op jit(solution)/shard_map/all_to_all | solution.py:119
  468.9 7.0 %all-to-all-start.13 = ((f32[4,1,256]{2,1,0:T(1,128)}), f32[4,1,256]{2,1,0:T(1,128)S(1)}, u32[]{:S(2)}, u32[]{:S(2)}) async-start(f32[4,1,256]{2,1,0:T(1,128)} %reshape.906), calls=%async_computation.13 | async-start | bytes 8192 | tf_op jit(solution)/shard_map/all_to_all | solution.py:105
  475.9 7.2 %all-to-all-start.17 = ((f32[4,1,256]{2,1,0:T(1,128)}), f32[4,1,256]{2,1,0:T(1,128)S(1)}, u32[]{:S(2)}, u32[]{:S(2)}) async-start(f32[4,1,256]{2,1,0:T(1,128)} %reshape.902), calls=%async_computation.17 | async-start | bytes 8192 | tf_op jit(solution)/shard_map/all_to_all | solution.py:118
  493.4 4.2 copy-start.4
Sparse Core Ops, SparseCore 0:
  27.7 62.8 all-gather.2
  309.1 35.6 all-gather.4
where the time goes:
time: 513 us; the launch traced here: 505 us
  other arithmetic  184 us (36%)
  waiting for transfers between devices  111 us (22%)
  local copies, waits for them, and re-layouts  84.3 us (16%)
  starting transfers between devices  66.6 us (13%)
  matrix products  44.7 us (9%)
  between operations  14.9 us (3%)
    gather x4, other arithmetic, shards(): pair_inv = point_inv[point_of_pair]  79.5 us
    sub x2, other arithmetic, shards(): pair_shift = point_max[point_of_pair] - coarse_shift  71.5 us
    all_to_all x1, waiting for transfers between devices, shards(): lax.all_to_all(outgoing, 'outer', split_axis=0, concat_axis=0, tiled=True)  57.9 us
    dot_general x2, matrix products, shards(): jnp.einsum('nbms,nbmd->bsd', weights, received, preferred_element_type=jn...  18 us
    dot_general x2, matrix products, shards(): jnp.einsum('nbmd,bsd->nbms', received, fine_now, preferred_element_type=j...  13.9 us
    all_to_all x1, waiting for transfers between devices, shards(): lax.all_to_all(lax.all_to_all(outgoing, 'outer', split_axis=0, concat_axi...  13.5 us
    unnamed x47, local copies, waits for them, and re-layouts  13.1 us
    gather x59, other arithmetic, shards(): pair_shift = point_max[point_of_pair] - coarse_shift  10.7 us
  transfers between devices with their start and end apart: 20, of which 14 were waited for; matrix products, arithmetic and copies ran while one was open for 28% of the time, Pallas kernels for 0%

commit v1 on v0

v1 whole, which is shorter than its diff:
```python
import functools
import math

import jax
import jax.numpy as jnp
from jax import lax
from jax.experimental import pallas as pl
from jax.experimental.pallas import tpu as pltpu
from jax.sharding import PartitionSpec as P

MOST = 2
ITERS = 2
PRIOR = 1.0
LOW = -3.0e38
AXES = ("outer", "bulk", "inner")
VMEM = 56 * 1024 * 1024


def pick_kernel(seg, ids_ref, x_ref, key_ref, xs_ref):
    blocks, lanes = key_ref.shape
    rows = xs_ref.shape[2]
    block = lax.broadcasted_iota(jnp.int32, (blocks, lanes), 0)
    pos = lax.broadcasted_iota(jnp.int32, (blocks, lanes), 1)
    member = jnp.zeros((blocks, lanes), jnp.int32)
    for k in range(ids_ref.shape[0]):
        member = jnp.where(ids_ref[k : k + 1, :] == block, 1, member)
    count = member
    inside = lax.rem(pos, seg)
    shift = 1
    while shift < seg:
        count = count + jnp.where(inside >= shift, pltpu.roll(count, shift, 1), 0)
        shift *= 2
    key = jnp.where(member == 1, (pos // seg) * MOST + count - member, -1)
    key_ref[...] = key
    row = lax.broadcasted_iota(jnp.int32, (rows, lanes), 0)
    group = max(1, min(blocks, 256 // rows))
    for g in range(0, blocks, group):
        hot = jnp.concatenate(
            [jnp.where(key[b : b + 1, :] == row, 1.0, 0.0) for b in range(g, g + group)], axis=0
        ).astype(jnp.bfloat16)
        got = jnp.dot(hot, x_ref[...], preferred_element_type=jnp.float32)
        xs_ref[0, g : g + group] = got.astype(jnp.bfloat16).reshape(group, rows, got.shape[1])


def lane_sum(x):
    total = x[:, :128]
    for j in range(128, x.shape[1], 128):
        total = total + x[:, j : j + 128]
    return total


def column(row):
    return jnp.broadcast_to(row, (128, 128)).T


def stats(fine, coarse, live, b, first, inv_root, key_ref, xs_ref, logit_ref, m_scr, s_scr, i):
    chunks, _, rows, _ = xs_ref.shape
    wide = fine.astype(jnp.float32)
    half = 0.5 * jnp.sum(lane_sum(wide * wide).T, axis=0, keepdims=True)
    cw = coarse.astype(jnp.float32)
    half_c = 0.5 * jnp.sum(cw * cw, axis=1, keepdims=True)
    lanes = key_ref.shape[1] // chunks
    row = lax.broadcasted_iota(jnp.int32, (rows, lanes), 0)
    for c in range(chunks):
        x = xs_ref[c, b]
        prod = lax.dot_general(
            x, fine, (((1,), (1,)), ((), ())), preferred_element_type=jnp.float32
        )
        shift = jnp.sum(lane_sum(x.astype(jnp.float32) * cw), axis=1, keepdims=True)
        logit = (prod - half) * inv_root + (shift - half_c) * inv_root
        logit = jnp.where(live == 1, logit, -jnp.inf)
        logit_ref[c, b] = logit
        m = jnp.max(logit, axis=1, keepdims=True)
        s = jnp.sum(jnp.exp(logit - m), axis=1, keepdims=True)
        part = pl.ds(c * lanes, lanes)
        hot = key_ref[b : b + 1, part] == row
        m_scr[i, b : b + 1, part] = jnp.sum(jnp.where(hot, m, 0.0), axis=0, keepdims=True)
        s_scr[i, b : b + 1, part] = jnp.sum(jnp.where(hot, s, 0.0), axis=0, keepdims=True)


def finish(keys_ref, m_scr, s_scr, stat_ref):
    steps, per, _ = m_scr.shape
    top = jnp.full((1, m_scr.shape[2]), LOW, jnp.float32)
    for i in range(steps):
        has = keys_ref[i] >= 0
        top = jnp.maximum(top, jnp.max(jnp.where(has, m_scr[i], LOW), axis=0, keepdims=True))
    total = jnp.zeros_like(top)
    for i in range(steps):
        has = keys_ref[i] >= 0
        term = s_scr[i] * jnp.exp(jnp.where(has, m_scr[i], LOW) - top)
        total = total + jnp.sum(jnp.where(has, term, 0.0), axis=0, keepdims=True)
    stat_ref[0:1, :] = top
    stat_ref[1:2, :] = total


def combine(all_ref, point_scr):
    top = all_ref[0, 0:1, :]
    for n in range(1, all_ref.shape[0]):
        top = jnp.maximum(top, all_ref[n, 0:1, :])
    total = jnp.zeros_like(top)
    for n in range(all_ref.shape[0]):
        total = total + all_ref[n, 1:2, :] * jnp.exp(all_ref[n, 0:1, :] - top)
    point_scr[0:1, :] = top
    point_scr[1:2, :] = 1.0 / total


def refresh(fine, live, b, key_ref, xs_ref, logit_ref, point_scr):
    chunks, _, rows, _ = xs_ref.shape
    lanes = key_ref.shape[1] // chunks
    row = lax.broadcasted_iota(jnp.int32, (rows, lanes), 0)
    mass = jnp.full((1, 128), PRIOR, jnp.float32)
    total = PRIOR * fine.astype(jnp.float32)
    for c in range(chunks):
        part = pl.ds(c * lanes, lanes)
        hot = key_ref[b : b + 1, part] == row
        top = jnp.sum(jnp.where(hot, point_scr[0:1, part], 0.0), axis=1, keepdims=True)
        inv = jnp.sum(jnp.where(hot, point_scr[1:2, part], 0.0), axis=1, keepdims=True)
        top = jnp.where(inv > 0.0, top, -LOW)
        w = (jnp.exp(logit_ref[c, b] - top) * inv).astype(jnp.bfloat16)
        mass = mass + jnp.sum(w.astype(jnp.float32), axis=0, keepdims=True)
        total = total + lax.dot_general(
            w, xs_ref[c, b], (((0,), (0,)), ((), ())), preferred_element_type=jnp.float32
        )
    recip = column(1.0 / mass)
    live_mass = jnp.where(live == 1, mass, 0.0)
    share = column(live_mass)
    news, sums = [], []
    for j in range(0, fine.shape[1], 128):
        new = (total[:, j : j + 128] * recip).astype(jnp.bfloat16)
        news.append(new)
        sums.append(jnp.sum(new.astype(jnp.float32) * share, axis=0, keepdims=True))
    coarse = jnp.concatenate(sums, axis=1) / jnp.sum(live_mass, axis=1, keepdims=True)
    return jnp.concatenate(news, axis=1), coarse.astype(jnp.bfloat16)


def first_kernel(inv_root, fine_ref, coarse_ref, live_ref, key_ref, keys_ref, xs_ref,
                 logit_ref, stat_ref, m_scr, s_scr):
    i = pl.program_id(0)
    for b in range(fine_ref.shape[0]):
        stats(fine_ref[b], coarse_ref[0, b : b + 1, :], live_ref[0, b : b + 1, :], b, 0, inv_root,
              key_ref.at[0], xs_ref, logit_ref, m_scr, s_scr, i)

    @pl.when(i == pl.num_programs(0) - 1)
    def _():
        finish(keys_ref, m_scr, s_scr, stat_ref)


def middle_kernel(inv_root, fine_ref, live_ref, key_ref, keys_ref, xs_ref, logit_ref, all_ref,
                  new_ref, out_logit_ref, stat_ref, m_scr, s_scr, point_scr):
    i = pl.program_id(0)

    @pl.when(i == 0)
    def _():
        combine(all_ref, point_scr)

    for b in range(fine_ref.shape[0]):
        live = live_ref[0, b : b + 1, :]
        fine, coarse = refresh(fine_ref[b], live, b, key_ref.at[0], xs_ref, logit_ref, point_scr)
        new_ref[b] = fine
        stats(fine, coarse, live, b, 0, inv_root, key_ref.at[0], xs_ref, out_logit_ref, m_scr,
              s_scr, i)

    @pl.when(i == pl.num_programs(0) - 1)
    def _():
        finish(keys_ref, m_scr, s_scr, stat_ref)


def last_kernel(fine_ref, live_ref, key_ref, xs_ref, logit_ref, all_ref, new_ref, coarse_ref,
                point_scr):
    i = pl.program_id(0)

    @pl.when(i == 0)
    def _():
        combine(all_ref, point_scr)

    for b in range(fine_ref.shape[0]):
        live = live_ref[0, b : b + 1, :]
        fine, coarse = refresh(fine_ref[b], live, b, key_ref.at[0], xs_ref, logit_ref, point_scr)
        new_ref[b] = fine
        coarse_ref[0, b : b + 1, :] = coarse


def spread_points(x):
    return lax.all_gather(x, AXES, axis=0, tiled=True)


def spread_stats(stat):
    return lax.all_gather(stat, AXES, axis=0, tiled=False)


def shards(points, coarse_ids, fine_cent, slot_live, coarse_cent):
    seg, top_count = coarse_ids.shape
    blocks, slots, feature = fine_cent.shape
    owners = lax.axis_size(AXES)
    me = lax.axis_index(AXES)
    total = owners * seg
    senders = min(owners, 16)
    chunks = owners // senders
    lanes = senders * seg
    rows = senders * MOST
    inv_root = 1.0 / math.sqrt(feature)
    per = min(blocks, 4)
    steps = blocks // per
    f32, bf16 = jnp.float32, jnp.bfloat16
    params = pltpu.CompilerParams(vmem_limit_bytes=VMEM, dimension_semantics=("arbitrary",))

    all_ids = lax.all_gather(coarse_ids, AXES, axis=0, tiled=True)
    rel_ids = all_ids.T - me * blocks
    all_points = spread_points(points)

    key, xs = pl.pallas_call(
        functools.partial(pick_kernel, seg),
        grid=(chunks,),
        in_specs=[
            pl.BlockSpec((top_count, lanes), lambda i: (0, i)),
            pl.BlockSpec((lanes, feature), lambda i: (i, 0)),
        ],
        out_specs=[
            pl.BlockSpec((blocks, lanes), lambda i: (0, i)),
            pl.BlockSpec((1, blocks, rows, feature), lambda i: (i, 0, 0, 0)),
        ],
        out_shape=[
            jax.ShapeDtypeStruct((blocks, total), jnp.int32),
            jax.ShapeDtypeStruct((chunks, blocks, rows, feature), bf16),
        ],
        compiler_params=params,
        name="pick",
    )(rel_ids, all_points)

    keys = key.reshape(steps, per, total)
    live = slot_live.reshape(steps, per, slots)
    coarse = coarse_cent.reshape(steps, per, feature)

    fine_spec = pl.BlockSpec((per, slots, feature), lambda i: (i, 0, 0))
    coarse_spec = pl.BlockSpec((1, per, feature), lambda i: (i, 0, 0))
    live_spec = pl.BlockSpec((1, per, slots), lambda i: (i, 0, 0))
    key_spec = pl.BlockSpec((1, per, total), lambda i: (i, 0, 0))
    keys_spec = pl.BlockSpec((steps, per, total), lambda i: (0, 0, 0))
    xs_spec = pl.BlockSpec((chunks, per, rows, feature), lambda i: (0, i, 0, 0))
    logit_spec = pl.BlockSpec((chunks, per, rows, slots), lambda i: (0, i, 0, 0))
    stat_spec = pl.BlockSpec((2, total), lambda i: (0, 0))
    all_spec = pl.BlockSpec((owners, 2, total), lambda i: (0, 0, 0))
    fine_shape = jax.ShapeDtypeStruct((blocks, slots, feature), bf16)
    logit_shape = jax.ShapeDtypeStruct((chunks, blocks, rows, slots), f32)
    stat_shape = jax.ShapeDtypeStruct((2, total), f32)
    grid_scr = pltpu.VMEM((steps, per, total), f32)
    point_scr = pltpu.VMEM((2, total), f32)

    logit, stat = pl.pallas_call(
        functools.partial(first_kernel, inv_root),
        grid=(steps,),
        in_specs=[fine_spec, coarse_spec, live_spec, key_spec, keys_spec, xs_spec],
        out_specs=[logit_spec, stat_spec],
        out_shape=[logit_shape, stat_shape],
        scratch_shapes=[grid_scr, grid_scr],
        compiler_params=params,
        name="first",
    )(fine_cent, coarse, live, keys, keys, xs)
    fine = fine_cent
    for _ in range(ITERS - 1):
        every = spread_stats(stat)
        fine, logit, stat = pl.pallas_call(
            functools.partial(middle_kernel, inv_root),
            grid=(steps,),
            in_specs=[fine_spec, live_spec, key_spec, keys_spec, xs_spec, logit_spec, all_spec],
            out_specs=[fine_spec, logit_spec, stat_spec],
            out_shape=[fine_shape, logit_shape, stat_shape],
            scratch_shapes=[grid_scr, grid_scr, point_scr],
            compiler_params=params,
            name="middle",
        )(fine, live, keys, keys, xs, logit, every)
    every = spread_stats(stat)
    fine, coarse = pl.pallas_call(
        last_kernel,
        grid=(steps,),
        in_specs=[fine_spec, live_spec, key_spec, xs_spec, logit_spec, all_spec],
        out_specs=[fine_spec, coarse_spec],
        out_shape=[fine_shape, jax.ShapeDtypeStruct((steps, per, feature), bf16)],
        scratch_shapes=[point_scr],
        compiler_params=params,
        name="last",
    )(fine, live, keys, xs, logit, every)
    return fine, coarse.reshape(blocks, feature)


def solution(mesh):
    spec = P(("groups",) + AXES)
    return jax.shard_map(
        shards, mesh=mesh, in_specs=(spec,) * 5, out_specs=(spec,) * 2, check_vma=False
    )
```

time: 513 us -> 155 us (0.30); the launches traced: 505 us -> 154 us
  other arithmetic: 184 us -> 0.01 us
  waiting for transfers between devices: 111 us -> 22.4 us
  local copies, waits for them, and re-layouts: 84.3 us -> 5.4 us
  starting transfers between devices: 66.6 us -> 0.04 us
  blocking collectives: 0 us -> 64.1 us
  Pallas kernels: 0 us -> 48.5 us
  matrix products: 44.7 us -> 0 us
    all_to_all x18 -> x0, waiting for transfers between devices: 110 us -> none  [the longest x1 57.9 us: shards(): lax.all_to_all(outgoing, 'outer', split_axis=0, concat_axis=0, tiled=True)]
    gather x66 -> x0, other arithmetic: 90.2 us -> none  [the longest x4 79.5 us: shards(): pair_inv = point_inv[point_of_pair]]
    sub x2 -> x1, other arithmetic: 71.5 us -> 0.01 us  [shards(): rel_ids = all_ids.T - me * blocks]
    all_to_all x18 -> x0, starting transfers between devices: 66.6 us -> none  [the longest x2 10.1 us: shards(): lax.all_to_all(inv_slots.reshape(outer_size, group_size, block_count * MO...]
    all_gather x0 -> x3, blocking collectives: none -> 64.1 us  [the longest x2 40.6 us: spread_stats(): return lax.all_gather(stat, AXES, axis=0, tiled=False)]
    pallas_call x0 -> x4, Pallas kernels: none -> 48.5 us  [the longest x1 17.7 us: shards(): pl.pallas_call(functools.partial(middle_kernel, inv_root), grid=(steps,),...]
    dot_general x8 -> x0, matrix products: 44.7 us -> none  [the longest x2 18 us: shards(): jnp.einsum('nbms,nbmd->bsd', weights, received, preferred_element_type=jn...]
    gather x29 -> x0, local copies, waits for them, and re-layouts: 42.3 us -> none  [the longest x2 10.3 us: shards(): picked = all_coarse[pair_ids].reshape(point_rows, top_count, feature)]
  transfers between devices with their start and end apart: 20 -> 1, of which waited for: 14 -> 1; matrix products, arithmetic and copies ran while one was open for 28% -> 1% of each run, Pallas kernels for 0% -> 0%
where the time goes in v1:
time: 155 us; the launch traced here: 154 us
  blocking collectives  64.1 us (41%)
  Pallas kernels  48.5 us (31%)
  waiting for transfers between devices  22.4 us (14%)
  between operations  14 us (9%)
  local copies, waits for them, and re-layouts  5.4 us (3%)
    all_gather x2, blocking collectives, spread_stats(): return lax.all_gather(stat, AXES, axis=0, tiled=False)  40.6 us
    all_gather x1, blocking collectives, shards(): all_ids = lax.all_gather(coarse_ids, AXES, axis=0, tiled=True)  23.5 us
    all_gather x1, waiting for transfers between devices, spread_points(): return lax.all_gather(x, AXES, axis=0, tiled=True)  21.7 us
    pallas_call x1, Pallas kernels, shards(): pl.pallas_call(functools.partial(middle_kernel, inv_root), grid=(steps,),...  17.7 us
    pallas_call x1, Pallas kernels, shards(): pl.pallas_call(last_kernel, grid=(steps,), in_specs=[fine_spec, live_spec...  13.3 us
    pallas_call x1, Pallas kernels, shards(): pl.pallas_call(functools.partial(first_kernel, inv_root), grid=(steps,),...  11 us
    pallas_call x1, Pallas kernels, shards(): pl.pallas_call(functools.partial(pick_kernel, seg), grid=(chunks,), in_sp...  6.42 us
  transfers between devices with their start and end apart: 1, of which 1 were waited for; matrix products, arithmetic and copies ran while one was open for 1% of the time, Pallas kernels for 0%

profile of v1, /device:TPU:0, one launch (start us, length us, event | category | flops | bytes accessed | tf_op | source)
XLA Modules:
  0.0 154.4 jit_solution(5726670909134603215)
XLA Ops:
  7.2 0.0 all-gather.7.cloned.1.call-start
  7.2 0.7 all-gather.7.cloned.1.call-update
  7.9 23.5 %all-gather.2 = s32[16,64,8]{1,2,0:T(8,128)S(1)} all-gather(s32[1,64,8]{1,2,0:T(8,128)} %bitcast.13), channel_id=1, replica_groups=mesh['groups'=2,'outer'=4,'bulk'=2,'inner'=2] {'outer','bulk','inner'}, dimensions={0}, use_global_device_ids=true | all-gather | bytes 34816 | tf_op jit(solution)/shard_map/all_gather | solution.py:207
  31.4 0.7 reshape.29
  32.1 1.5 reshape.18.coarse_ref
  33.7 21.7 %all-gather.7.cloned.1.call-done.x_ref = bf16[1024,1152]{1,0:T(8,128)(2,1)} async-done(((bf16[64,1152]{1,0:T(8,128)(2,1)}), bf16[1024,1152]{1,0:T(8,128)(2,1)}) %all-gather.7.cloned.1.call-update) | async-done | bytes 2359312 | tf_op jit(solution)/shard_map/all_gather | solution.py:184
  55.4 6.4 %pick.1 = (s32[32,1024]{1,0:T(8,128)}, bf16[1,32,32,1152]{3,2,1,0:T(8,128)(2,1)}) custom-call(s32[8,1024]{1,0:T(8,128)} %bitcast.10, bf16[1024,1152]{1,0:T(8,128)(2,1)} %all-gather.7.cloned.1.call-done.x_ref), custom_call_target="tpu_custom_call" | custom-call | tf_op jit(solution)/shard_map/pick/pallas_call | solution.py:211
  61.8 1.6 %reshape.17.key_ref.keys_ref = s32[8,4,1024]{2,1,0:T(4,128)} reshape(s32[32,1024]{1,0:T(8,128)} %get-tuple-element.11) | data formatting | bytes 262144 | tf_op jit(solution)/shard_map/reshape | solution.py:230
  63.4 11.0 %first.1 = (f32[1,32,32,128]{3,2,1,0:T(8,128)}, f32[2,1024]{1,0:T(2,128)}) custom-call(bf16[32,128,1152]{2,1,0:T(8,128)(2,1)} %fine_ref.3, bf16[8,4,1152]{2,1,0:T(4,128)(2,1)} %reshape.18.coarse_ref, s32[8,4,128]{2,1,0:T(4,128)} %bitcast.7, s32[8,4,1024]{2,1,0:T(4,128)} %reshape.17.key_ref.keys_ref, s32[8,4,1024]{2,1,0:T(4,128)} %reshape.17.key_ref.keys_ref, ...), custom_call_target="tpu_custom_call" | custom-call | tf_op jit(solution)/shard_map/first/pallas_call | solution.py:249
  74.4 21.2 %all-gather.3.all_ref = f32[16,2,1024]{2,1,0:T(2,128)} all-gather(f32[1,2,1024]{2,1,0:T(2,128)} %bitcast.12), channel_id=2, replica_groups=mesh['groups'=2,'outer'=4,'bulk'=2,'inner'=2] {'outer','bulk','inner'}, dimensions={0}, use_global_device_ids=true | all-gather | bytes 139264 | tf_op jit(solution)/shard_map/all_gather | solution.py:188
  95.6 17.7 %middle.1 = (bf16[32,128,1152]{2,1,0:T(8,128)(2,1)}, f32[1,32,32,128]{3,2,1,0:T(8,128)}, f32[2,1024]{1,0:T(2,128)}) custom-call(bf16[32,128,1152]{2,1,0:T(8,128)(2,1)} %fine_ref.3, s32[8,4,128]{2,1,0:T(4,128)} %bitcast.8, s32[8,4,1024]{2,1,0:T(4,128)} %reshape.17.key_ref.keys_ref, s32[8,4,1024]{2,1,0:T(4,128)} %reshape.17.key_ref.keys_ref, ...), custom_call_target="tpu_custom_call" | custom-call | tf_op jit(solution)/shard_map/middle/pallas_call | solution.py:262
  113.3 19.4 %all-gather.4.all_ref = f32[16,2,1024]{2,1,0:T(2,128)} all-gather(f32[1,2,1024]{2,1,0:T(2,128)} %bitcast.11), channel_id=3, replica_groups=mesh['groups'=2,'outer'=4,'bulk'=2,'inner'=2] {'outer','bulk','inner'}, dimensions={0}, use_global_device_ids=true | all-gather | bytes 139264 | tf_op jit(solution)/shard_map/all_gather | solution.py:188
  132.7 13.3 %last.1 = (bf16[32,128,1152]{2,1,0:T(8,128)(2,1)}, bf16[8,4,1152]{2,1,0:T(4,128)(2,1)}) custom-call(bf16[32,128,1152]{2,1,0:T(8,128)(2,1)} %get-tuple-element.15.fine_ref, s32[8,4,128]{2,1,0:T(4,128)} %bitcast.9, s32[8,4,1024]{2,1,0:T(4,128)} %reshape.17.key_ref.keys_ref, bf16[1,32,32,1152]{3,2,1,0:T(8,128)(2,1)} %get-tuple-element.12.xs_ref, ...), custom_call_target="tpu_custom_call" | custom-call | tf_op jit(solution)/shard_map/last/pallas_call | solution.py:273
  146.0 1.5 reshape.19
  (2 shorter events, 0.0 us)
Async XLA Ops:
  7.2 48.2 %all-gather.7.cloned.1.call-start = ((), (), s32[]{:S(2)}) async-start(), calls=%async_computation | async-start | bytes 2506752 | tf_op jit(solution)/shard_map/all_gather | solution.py:184
Sparse Core Ops, SparseCore 0:
  10.3 45.0 all-gather.6

commit v2 on v1

v2 whole, which is shorter than its diff:
```python
import functools
import math

import jax
import jax.numpy as jnp
from jax import lax
from jax.experimental import pallas as pl
from jax.experimental.pallas import tpu as pltpu
from jax.sharding import PartitionSpec as P

MOST = 2
ITERS = 2
PRIOR = 1.0
LOW = -3.0e38
AXES = ("outer", "bulk", "inner")
VMEM = 56 * 1024 * 1024


def pick_kernel(seg, ids_ref, x_ref, key_ref, xs_ref):
    blocks, lanes = key_ref.shape
    rows = xs_ref.shape[2]
    block = lax.broadcasted_iota(jnp.int32, (blocks, lanes), 0)
    pos = lax.broadcasted_iota(jnp.int32, (blocks, lanes), 1)
    z, x, c = [lax.axis_index(a) for a in AXES]
    me = (z * lax.axis_size("bulk") + x) * lax.axis_size("inner") + c
    pack = 128 // seg
    part = lax.broadcasted_iota(jnp.int32, ids_ref.shape[1:], 1) // seg
    tiles = []
    for j in range(0, ids_ref.shape[0], pack):
        tile = ids_ref[j]
        for q in range(1, pack):
            tile = jnp.where(part == q, ids_ref[j + q], tile)
        tiles.append(tile)
    ids = jnp.concatenate(tiles, axis=1) - me * blocks
    member = jnp.zeros((blocks, lanes), jnp.int32)
    for k in range(ids.shape[0]):
        member = jnp.where(ids[k : k + 1, :] == block, 1, member)
    count = member
    inside = lax.rem(pos, seg)
    shift = 1
    while shift < seg:
        count = count + jnp.where(inside >= shift, pltpu.roll(count, shift, 1), 0)
        shift *= 2
    key = jnp.where(member == 1, (pos // seg) * MOST + count - member, -1)
    key_ref[...] = key
    row = lax.broadcasted_iota(jnp.int32, (rows, lanes), 0)
    group = max(1, min(blocks, 256 // rows))
    for g in range(0, blocks, group):
        hot = jnp.concatenate(
            [jnp.where(key[b : b + 1, :] == row, 1.0, 0.0) for b in range(g, g + group)], axis=0
        ).astype(jnp.bfloat16)
        got = jnp.dot(hot, x_ref[...], preferred_element_type=jnp.float32)
        xs_ref[0, g : g + group] = got.astype(jnp.bfloat16).reshape(group, rows, got.shape[1])


def lane_sum(x):
    total = x[:, :128]
    for j in range(128, x.shape[1], 128):
        total = total + x[:, j : j + 128]
    return total


def column(row):
    return jnp.broadcast_to(row, (128, 128)).T


def stats(fine, cw, live, b, n, inv_root, key_ref, xs_ref, logit_ref, m_scr, s_scr):
    chunks, _, rows, _ = xs_ref.shape
    wide = fine.astype(jnp.float32)
    half = 0.5 * jnp.sum(lane_sum(wide * wide).T, axis=0, keepdims=True)
    half_c = 0.5 * jnp.sum(cw * cw, axis=1, keepdims=True)
    lanes = key_ref.shape[1] // chunks
    row = lax.broadcasted_iota(jnp.int32, (rows, lanes), 0)
    for c in range(chunks):
        x = xs_ref[c, b]
        prod = lax.dot_general(
            x, fine, (((1,), (1,)), ((), ())), preferred_element_type=jnp.float32
        )
        shift = jnp.sum(lane_sum(x.astype(jnp.float32) * cw), axis=1, keepdims=True)
        logit = (prod - half) * inv_root + (shift - half_c) * inv_root
        logit = jnp.where(live == 1, logit, -jnp.inf)
        logit_ref[c, b] = logit
        m = jnp.max(logit, axis=1, keepdims=True)
        s = jnp.sum(jnp.exp(logit - m), axis=1, keepdims=True)
        part = pl.ds(c * lanes, lanes)
        hot = key_ref[pl.ds(n, 1), part] == row
        m_scr[pl.ds(n, 1), part] = jnp.sum(jnp.where(hot, m, 0.0), axis=0, keepdims=True)
        s_scr[pl.ds(n, 1), part] = jnp.sum(jnp.where(hot, s, 0.0), axis=0, keepdims=True)


def finish(key_ref, m_scr, s_scr, stat_ref):
    has = key_ref[...] >= 0
    large = jnp.where(has, m_scr[...], LOW)
    top = jnp.max(large, axis=0, keepdims=True)
    term = s_scr[...] * jnp.exp(large - top)
    stat_ref[0:1, :] = top
    stat_ref[1:2, :] = jnp.sum(jnp.where(has, term, 0.0), axis=0, keepdims=True)


def combine(all_ref, point_scr):
    top = all_ref[0, 0:1, :]
    for n in range(1, all_ref.shape[0]):
        top = jnp.maximum(top, all_ref[n, 0:1, :])
    total = jnp.zeros_like(top)
    for n in range(all_ref.shape[0]):
        total = total + all_ref[n, 1:2, :] * jnp.exp(all_ref[n, 0:1, :] - top)
    point_scr[0:1, :] = top
    point_scr[1:2, :] = 1.0 / total


def refresh(fine, live, b, n, key_ref, xs_ref, logit_ref, point_scr):
    chunks, _, rows, _ = xs_ref.shape
    lanes = key_ref.shape[1] // chunks
    row = lax.broadcasted_iota(jnp.int32, (rows, lanes), 0)
    mass = jnp.full((1, 128), PRIOR, jnp.float32)
    total = PRIOR * fine.astype(jnp.float32)
    for c in range(chunks):
        part = pl.ds(c * lanes, lanes)
        hot = key_ref[pl.ds(n, 1), part] == row
        top = jnp.sum(jnp.where(hot, point_scr[0:1, part], 0.0), axis=1, keepdims=True)
        inv = jnp.sum(jnp.where(hot, point_scr[1:2, part], 0.0), axis=1, keepdims=True)
        top = jnp.where(inv > 0.0, top, -LOW)
        w = (jnp.exp(logit_ref[c, b] - top) * inv).astype(jnp.bfloat16)
        mass = mass + jnp.sum(w.astype(jnp.float32), axis=0, keepdims=True)
        total = total + lax.dot_general(
            w, xs_ref[c, b], (((0,), (0,)), ((), ())), preferred_element_type=jnp.float32
        )
    recip = column(1.0 / mass)
    live_mass = jnp.where(live == 1, mass, 0.0)
    share = column(live_mass)
    news, sums = [], []
    for j in range(0, fine.shape[1], 128):
        new = (total[:, j : j + 128] * recip).astype(jnp.bfloat16)
        news.append(new)
        sums.append(jnp.sum(new.astype(jnp.float32) * share, axis=0, keepdims=True))
    coarse = jnp.concatenate(sums, axis=1) / jnp.sum(live_mass, axis=1, keepdims=True)
    return jnp.concatenate(news, axis=1), coarse.astype(jnp.bfloat16)


def first_kernel(inv_root, fine_ref, coarse_ref, live_ref, key_ref, xs_ref, logit_ref, stat_ref,
                 m_scr, s_scr, coarse_scr):
    i = pl.program_id(0)
    per = fine_ref.shape[0]

    @pl.when(i == 0)
    def _():
        coarse_scr[...] = coarse_ref[...].astype(jnp.float32)

    for b in range(per):
        n = i * per + b
        stats(fine_ref[b], coarse_scr[pl.ds(n, 1), :], live_ref[pl.ds(n, 1), :], b, n, inv_root,
              key_ref, xs_ref, logit_ref, m_scr, s_scr)

    @pl.when(i == pl.num_programs(0) - 1)
    def _():
        finish(key_ref, m_scr, s_scr, stat_ref)


def middle_kernel(inv_root, fine_ref, live_ref, key_ref, xs_ref, logit_ref, all_ref,
                  new_ref, out_logit_ref, stat_ref, m_scr, s_scr, point_scr):
    i = pl.program_id(0)
    per = fine_ref.shape[0]

    @pl.when(i == 0)
    def _():
        combine(all_ref, point_scr)

    for b in range(per):
        n = i * per + b
        live = live_ref[pl.ds(n, 1), :]
        fine, coarse = refresh(fine_ref[b], live, b, n, key_ref, xs_ref, logit_ref, point_scr)
        new_ref[b] = fine
        stats(fine, coarse.astype(jnp.float32), live, b, n, inv_root, key_ref, xs_ref,
              out_logit_ref, m_scr, s_scr)

    @pl.when(i == pl.num_programs(0) - 1)
    def _():
        finish(key_ref, m_scr, s_scr, stat_ref)


def last_kernel(fine_ref, live_ref, key_ref, xs_ref, logit_ref, all_ref, new_ref, coarse_ref,
                point_scr, coarse_scr):
    i = pl.program_id(0)
    per = fine_ref.shape[0]

    @pl.when(i == 0)
    def _():
        combine(all_ref, point_scr)

    for b in range(per):
        n = i * per + b
        live = live_ref[pl.ds(n, 1), :]
        fine, coarse = refresh(fine_ref[b], live, b, n, key_ref, xs_ref, logit_ref, point_scr)
        new_ref[b] = fine
        coarse_scr[pl.ds(n, 1), :] = coarse.astype(jnp.float32)

    @pl.when(i == pl.num_programs(0) - 1)
    def _():
        coarse_ref[...] = coarse_scr[...].astype(jnp.bfloat16)


MESH = pl.DeviceIdType.MESH


def place():
    _, width, cores = [lax.axis_size(a) for a in AXES]
    group = lax.axis_index("groups")
    z, x, c = [lax.axis_index(a) for a in AXES]

    def device(n):
        return (group, n // (width * cores), lax.rem(n // cores, width), lax.rem(n, cores))

    return (z * width + x) * cores + c, device


def greet(owners, me, device):
    barrier = pltpu.get_barrier_semaphore()

    def hello(d, carry):
        peer = lax.rem(me + d, owners)
        pl.semaphore_signal(barrier, inc=1, device_id=device(peer), device_id_type=MESH)
        return carry

    lax.fori_loop(1, owners, hello, 0)
    pl.semaphore_wait(barrier, owners - 1)


def direct(owners, me, device, src, dst, send_sem, recv_sem):
    def copy(peer, slot):
        return pltpu.make_async_remote_copy(
            src_ref=src, dst_ref=dst.at[slot], send_sem=send_sem.at[peer],
            recv_sem=recv_sem.at[slot], device_id=device(peer), device_id_type=MESH,
        )

    def start(d, carry):
        copy(lax.rem(me + d, owners), me).start()
        return carry

    def wait(d, carry):
        peer = lax.rem(me + d, owners)
        copy(peer, peer).wait_recv()
        copy(peer, me).wait_send()
        return carry

    return (lambda: lax.fori_loop(1, owners, start, 0)), (
        lambda: lax.fori_loop(1, owners, wait, 0)
    )


def exchange_kernel(owners, src_ref, dst_ref, send_sem, recv_sem, own_sem):
    me, device = place()
    own = pltpu.make_async_copy(src_ref, dst_ref.at[me], own_sem)
    own.start()
    greet(owners, me, device)
    start, wait = direct(owners, me, device, src_ref, dst_ref, send_sem, recv_sem)
    start()
    own.wait()
    wait()


def spread_stats(stat):
    owners = lax.axis_size(AXES)
    return pl.pallas_call(
        functools.partial(exchange_kernel, owners),
        in_specs=[pl.BlockSpec(memory_space=pl.ANY)],
        out_specs=pl.BlockSpec(memory_space=pl.ANY),
        out_shape=jax.ShapeDtypeStruct((owners,) + stat.shape, stat.dtype),
        scratch_shapes=[
            pltpu.SemaphoreType.DMA((owners,)),
            pltpu.SemaphoreType.DMA((owners,)),
            pltpu.SemaphoreType.DMA,
        ],
        compiler_params=pltpu.CompilerParams(collective_id=1, has_side_effects=True),
        name="exchange",
    )(stat)


def gather_kernel(x_ref, ids_ref, out_ref, ids_out_ref, z_send, x_send, c_send, recv, ids_send,
                  ids_recv, own_sem):
    depth, width, cores = [lax.axis_size(a) for a in AXES]
    owners = depth * width * cores
    group = lax.axis_index("groups")
    z, x, c = [lax.axis_index(a) for a in AXES]
    me, device = place()

    def slot_of(zz, xx, cc):
        return (zz * width + xx) * cores + cc

    own = pltpu.make_async_copy(x_ref, out_ref.at[me], own_sem.at[0])
    own.start()
    own_ids = pltpu.make_async_copy(ids_ref, ids_out_ref.at[me], own_sem.at[1])
    own_ids.start()
    greet(owners, me, device)

    def copy(src, slot, sem, target):
        return pltpu.make_async_remote_copy(
            src_ref=src, dst_ref=out_ref.at[slot], send_sem=sem, recv_sem=recv.at[slot],
            device_id=target, device_id_type=MESH,
        )

    def arrive(slot):
        copy(x_ref, slot, own_sem.at[0], (group, z, x, c)).wait_recv()

    def along_z(src, zz, step):
        side = 0 if step > 0 else 1
        return copy(src, slot_of(zz, x, c), z_send.at[side, zz], (group, z + step, x, c))

    def along_x(src, zz, e):
        return copy(
            src, slot_of(zz, x, c), x_send.at[e, zz], (group, z, lax.rem(x + e, width), c)
        )

    def along_c(src, zz, xx, e):
        return copy(
            src, slot_of(zz, xx, c), c_send.at[e, zz * width + xx],
            (group, z, x, lax.rem(c + e, cores)),
        )

    def spread(src, zz):
        for e in range(1, width):
            along_x(src, zz, e).start()
        for e in range(1, cores):
            along_c(src, zz, x, e).start()

    def from_x(zz):
        for e in range(1, width):
            xx = lax.rem(x + e, width)
            slot = slot_of(zz, xx, c)
            arrive(slot)
            for f in range(1, cores):
                along_c(out_ref.at[slot], zz, xx, f).start()

    @pl.when(z + 1 < depth)
    def _():
        along_z(x_ref, z, 1).start()

    @pl.when(z > 0)
    def _():
        along_z(x_ref, z, -1).start()

    spread(x_ref, z)
    start_ids, wait_ids = direct(owners, me, device, ids_ref, ids_out_ref, ids_send, ids_recv)
    start_ids()

    def step(t, carry):
        for sign in (1, -1):
            zz = z - sign * t
            known = (zz >= 0) & (zz < depth)
            onward = (z + sign >= 0) & (z + sign < depth)

            @pl.when(known)
            def _():
                slot = slot_of(zz, x, c)
                arrive(slot)

                @pl.when(onward)
                def _():
                    along_z(out_ref.at[slot], zz, sign).start()

                spread(out_ref.at[slot], zz)

        for sign in (1, -1):
            zz = z - sign * (t - 1)

            @pl.when((zz >= 0) & (zz < depth) & ((t > 1) | (sign == 1)))
            def _():
                from_x(zz)

        return carry

    lax.fori_loop(1, depth, step, 0)
    for sign in (1, -1):
        zz = z - sign * (depth - 1)

        @pl.when((zz >= 0) & (zz < depth))
        def _():
            from_x(zz)

    def last(zz, carry):
        for e in range(1, cores):
            for xx in range(width):
                arrive(slot_of(zz, xx, lax.rem(c + e, cores)))
        return carry

    lax.fori_loop(0, depth, last, 0)
    wait_ids()

    def sent(zz, carry):
        @pl.when((zz <= z) & (z + 1 < depth))
        def _():
            along_z(x_ref, zz, 1).wait_send()

        @pl.when((zz >= z) & (z > 0))
        def _():
            along_z(x_ref, zz, -1).wait_send()

        for e in range(1, width):
            along_x(x_ref, zz, e).wait_send()
        for e in range(1, cores):
            for xx in range(width):
                along_c(x_ref, zz, xx, e).wait_send()
        return carry

    lax.fori_loop(0, depth, sent, 0)
    own.wait()
    own_ids.wait()


def spread_points(points, ids):
    depth, width, cores = [lax.axis_size(a) for a in AXES]
    owners = depth * width * cores
    return pl.pallas_call(
        gather_kernel,
        in_specs=[pl.BlockSpec(memory_space=pl.ANY)] * 2,
        out_specs=[pl.BlockSpec(memory_space=pl.ANY)] * 2,
        out_shape=[
            jax.ShapeDtypeStruct((owners,) + points.shape, points.dtype),
            jax.ShapeDtypeStruct((owners,) + ids.shape, ids.dtype),
        ],
        scratch_shapes=[
            pltpu.SemaphoreType.DMA((2, depth)),
            pltpu.SemaphoreType.DMA((width, depth)),
            pltpu.SemaphoreType.DMA((cores, depth * width)),
            pltpu.SemaphoreType.DMA((owners,)),
            pltpu.SemaphoreType.DMA((owners,)),
            pltpu.SemaphoreType.DMA((owners,)),
            pltpu.SemaphoreType.DMA((2,)),
        ],
        compiler_params=pltpu.CompilerParams(collective_id=0, has_side_effects=True),
        name="gather",
    )(points, ids)


def shards(points, coarse_ids, fine_cent, slot_live, coarse_cent):
    seg, top_count = coarse_ids.shape
    blocks, slots, feature = fine_cent.shape
    owners = lax.axis_size(AXES)
    total = owners * seg
    senders = min(owners, 16)
    chunks = owners // senders
    lanes = senders * seg
    rows = senders * MOST
    inv_root = 1.0 / math.sqrt(feature)
    per = min(blocks, 4)
    steps = blocks // per
    f32, bf16 = jnp.float32, jnp.bfloat16
    params = pltpu.CompilerParams(vmem_limit_bytes=VMEM, dimension_semantics=("arbitrary",))

    ids = jnp.concatenate([coarse_ids.T] * (128 // seg), axis=1)
    all_points, all_ids = spread_points(points, ids)
    all_points = all_points.reshape(total, feature)

    key, xs = pl.pallas_call(
        functools.partial(pick_kernel, seg),
        grid=(chunks,),
        in_specs=[
            pl.BlockSpec((senders, top_count, 128), lambda i: (i, 0, 0)),
            pl.BlockSpec((lanes, feature), lambda i: (i, 0)),
        ],
        out_specs=[
            pl.BlockSpec((blocks, lanes), lambda i: (0, i)),
            pl.BlockSpec((1, blocks, rows, feature), lambda i: (i, 0, 0, 0)),
        ],
        out_shape=[
            jax.ShapeDtypeStruct((blocks, total), jnp.int32),
            jax.ShapeDtypeStruct((chunks, blocks, rows, feature), bf16),
        ],
        compiler_params=params,
        name="pick",
    )(all_ids, all_points)

    fine_spec = pl.BlockSpec((per, slots, feature), lambda i: (i, 0, 0))
    coarse_spec = pl.BlockSpec((blocks, feature), lambda i: (0, 0))
    live_spec = pl.BlockSpec((blocks, slots), lambda i: (0, 0))
    key_spec = pl.BlockSpec((blocks, total), lambda i: (0, 0))
    xs_spec = pl.BlockSpec((chunks, per, rows, feature), lambda i: (0, i, 0, 0))
    logit_spec = pl.BlockSpec((chunks, per, rows, slots), lambda i: (0, i, 0, 0))
    stat_spec = pl.BlockSpec((2, total), lambda i: (0, 0))
    all_spec = pl.BlockSpec((owners, 2, total), lambda i: (0, 0, 0))
    fine_shape = jax.ShapeDtypeStruct((blocks, slots, feature), bf16)
    logit_shape = jax.ShapeDtypeStruct((chunks, blocks, rows, slots), f32)
    stat_shape = jax.ShapeDtypeStruct((2, total), f32)
    grid_scr = pltpu.VMEM((blocks, total), f32)
    coarse_scr = pltpu.VMEM((blocks, feature), f32)
    point_scr = pltpu.VMEM((2, total), f32)

    logit, stat = pl.pallas_call(
        functools.partial(first_kernel, inv_root),
        grid=(steps,),
        in_specs=[fine_spec, coarse_spec, live_spec, key_spec, xs_spec],
        out_specs=[logit_spec, stat_spec],
        out_shape=[logit_shape, stat_shape],
        scratch_shapes=[grid_scr, grid_scr, coarse_scr],
        compiler_params=params,
        name="first",
    )(fine_cent, coarse_cent, slot_live, key, xs)
    fine = fine_cent
    for _ in range(ITERS - 1):
        every = spread_stats(stat)
        fine, logit, stat = pl.pallas_call(
            functools.partial(middle_kernel, inv_root),
            grid=(steps,),
            in_specs=[fine_spec, live_spec, key_spec, xs_spec, logit_spec, all_spec],
            out_specs=[fine_spec, logit_spec, stat_spec],
            out_shape=[fine_shape, logit_shape, stat_shape],
            scratch_shapes=[grid_scr, grid_scr, point_scr],
            compiler_params=params,
            name="middle",
        )(fine, slot_live, key, xs, logit, every)
    every = spread_stats(stat)
    fine, coarse = pl.pallas_call(
        last_kernel,
        grid=(steps,),
        in_specs=[fine_spec, live_spec, key_spec, xs_spec, logit_spec, all_spec],
        out_specs=[fine_spec, coarse_spec],
        out_shape=[fine_shape, jax.ShapeDtypeStruct((blocks, feature), bf16)],
        scratch_shapes=[point_scr, coarse_scr],
        compiler_params=params,
        name="last",
    )(fine, slot_live, key, xs, logit, every)
    return fine, coarse


def solution(mesh):
    spec = P(("groups",) + AXES)
    return jax.shard_map(
        shards, mesh=mesh, in_specs=(spec,) * 5, out_specs=(spec,) * 2, check_vma=False
    )
```

time: 155 us -> 93.3 us (0.60)
  blocking collectives: 64.1 us -> 0 us
  Pallas kernels: 48.5 us -> 90.5 us
  waiting for transfers between devices: 22.4 us -> 0 us
  between operations: 14 us -> 0.66 us
  local copies, waits for them, and re-layouts: 5.4 us -> 0 us
    all_gather x3 -> x0, blocking collectives: 64.1 us -> none  [the longest x2 40.6 us: spread_stats(): return lax.all_gather(stat, AXES, axis=0, tiled=False)]
    pallas_call x0 -> x3, Pallas kernels: none -> 42.8 us  [the longest x1 26.5 us: spread_points(): pl.pallas_call(gather_kernel, in_specs=[pl.BlockSpec(memory_space=pl.ANY)...]
    all_gather x1 -> x0, waiting for transfers between devices: 21.7 us -> none  [spread_points(): return lax.all_gather(x, AXES, axis=0, tiled=True)]
    reshape x3 -> x0, local copies, waits for them, and re-layouts: 4.69 us -> none  [the longest x1 1.62 us: shards(): keys = key.reshape(steps, per, total)]
  transfers between devices with their start and end apart: 1 -> 0, of which waited for: 1 -> 0; matrix products, arithmetic and copies ran while one was open for 1% -> 0% of each run, Pallas kernels for 0% -> 0%
where the time goes in v2:
time: 93.3 us; the launch traced here: 92.5 us
  Pallas kernels  90.5 us (97%)
  other arithmetic  1.43 us (2%)
    pallas_call x1, Pallas kernels, spread_points(): pl.pallas_call(gather_kernel, in_specs=[pl.BlockSpec(memory_space=pl.ANY)...  26.5 us
    pallas_call x1, Pallas kernels, shards(): pl.pallas_call(functools.partial(middle_kernel, inv_root), grid=(steps,),...  17.3 us
    pallas_call x2, Pallas kernels, spread_stats(): pl.pallas_call(functools.partial(exchange_kernel, owners), in_specs=[pl.B...  16.3 us
    pallas_call x1, Pallas kernels, shards(): pl.pallas_call(last_kernel, grid=(steps,), in_specs=[fine_spec, live_spec...  13.4 us
    pallas_call x1, Pallas kernels, shards(): pl.pallas_call(functools.partial(first_kernel, inv_root), grid=(steps,),...  10.5 us
    pallas_call x1, Pallas kernels, shards(): pl.pallas_call(functools.partial(pick_kernel, seg), grid=(chunks,), in_sp...  6.47 us

profile of v2, /device:TPU:0, one launch (start us, length us, event | category | flops | bytes accessed | tf_op | source)
XLA Modules:
  0.0 92.5 jit_solution(9659118661885778026)
XLA Ops:
  0.6 1.4 %pad_add_fusion.ids_ref = s32[8,128]{1,0:T(8,128)} fusion(s32[8,64]{1,0:T(8,128)} %bitcast.3), kind=kLoop, calls=%fused_computation | loop fusion | flops 1024 | bytes 6144 | tf_op jit(solution)/shard_map/concatenate | solution.py:449
  2.1 26.5 %gather.1 = (bf16[16,64,1152]{2,1,0:T(8,128)(2,1)}, s32[16,8,128]{2,1,0:T(8,128)}) custom-call(bf16[64,1152]{1,0:T(8,128)(2,1)} %x_ref.1, s32[8,128]{1,0:T(8,128)} %pad_add_fusion.ids_ref), custom_call_target="tpu_custom_call" | custom-call | tf_op jit(solution)/shard_map/gather/pallas_call | solution.py:412
  28.6 6.5 %pick.1 = (s32[32,1024]{1,0:T(8,128)}, bf16[1,32,32,1152]{3,2,1,0:T(8,128)(2,1)}) custom-call(s32[16,8,128]{2,1,0:T(8,128)} %get-tuple-element.11.ids_ref, bf16[1024,1152]{1,0:T(8,128)(2,1)} %bitcast.2), custom_call_target="tpu_custom_call" | custom-call | tf_op jit(solution)/shard_map/pick/pallas_call | solution.py:453
  35.1 10.5 %first.1 = (f32[1,32,32,128]{3,2,1,0:T(8,128)}, f32[2,1024]{1,0:T(2,128)}) custom-call(bf16[32,128,1152]{2,1,0:T(8,128)(2,1)} %fine_ref.3, bf16[32,1152]{1,0:T(8,128)(2,1)} %coarse_ref.1, s32[32,128]{1,0:T(8,128)} %live_ref.5, s32[32,1024]{1,0:T(8,128)} %get-tuple-element.13.key_ref, bf16[1,32,32,1152]{3,2,1,0:T(8,128)(2,1)} %get-tuple-element.14.xs_ref), custom_call_target="tpu_custom_call" | custom-call | tf_op jit(solution)/shard_map/first/pallas_call | solution.py:487
  45.5 7.6 %exchange.2.all_ref = f32[16,2,1024]{2,1,0:T(2,128)} custom-call(f32[2,1024]{1,0:T(2,128)} %get-tuple-element.16.src_ref), custom_call_target="tpu_custom_call" | custom-call | tf_op jit(solution)/shard_map/exchange/pallas_call | solution.py:263
  53.1 17.3 %middle.1 = (bf16[32,128,1152]{2,1,0:T(8,128)(2,1)}, f32[1,32,32,128]{3,2,1,0:T(8,128)}, f32[2,1024]{1,0:T(2,128)}) custom-call(bf16[32,128,1152]{2,1,0:T(8,128)(2,1)} %fine_ref.3, s32[32,128]{1,0:T(8,128)} %live_ref.5, s32[32,1024]{1,0:T(8,128)} %get-tuple-element.13.key_ref, bf16[1,32,32,1152]{3,2,1,0:T(8,128)(2,1)} %get-tuple-element.14.xs_ref, ...), custom_call_target="tpu_custom_call" | custom-call | tf_op jit(solution)/shard_map/middle/pallas_call | solution.py:500
  70.4 8.7 %exchange.3.all_ref = f32[16,2,1024]{2,1,0:T(2,128)} custom-call(f32[2,1024]{1,0:T(2,128)} %get-tuple-element.19.src_ref), custom_call_target="tpu_custom_call" | custom-call | tf_op jit(solution)/shard_map/exchange/pallas_call | solution.py:263
  79.1 13.4 %last.1 = (bf16[32,128,1152]{2,1,0:T(8,128)(2,1)}, bf16[32,1152]{1,0:T(8,128)(2,1)}) custom-call(bf16[32,128,1152]{2,1,0:T(8,128)(2,1)} %get-tuple-element.17.fine_ref, s32[32,128]{1,0:T(8,128)} %live_ref.5, s32[32,1024]{1,0:T(8,128)} %get-tuple-element.13.key_ref, bf16[1,32,32,1152]{3,2,1,0:T(8,128)(2,1)} %get-tuple-element.14.xs_ref, ...), custom_call_target="tpu_custom_call" | custom-call | tf_op jit(solution)/shard_map/last/pallas_call | solution.py:511

commit v3 on v2

v3 whole, which is shorter than its diff:
```python
import functools
import math

import jax
import jax.numpy as jnp
from jax import lax
from jax.experimental import pallas as pl
from jax.experimental.pallas import tpu as pltpu
from jax.sharding import PartitionSpec as P

MOST = 2
ITERS = 2
PRIOR = 1.0
LOW = -3.0e38
HALVES = 2
PER = 8
AXES = ("outer", "bulk", "inner")
VMEM = 56 * 1024 * 1024


def pick_kernel(seg, ids_ref, x_ref, key_ref, xs_ref):
    blocks, lanes = key_ref.shape
    rows = xs_ref.shape[2]
    block = lax.broadcasted_iota(jnp.int32, (blocks, lanes), 0)
    pos = lax.broadcasted_iota(jnp.int32, (blocks, lanes), 1)
    z, x, c = [lax.axis_index(a) for a in AXES]
    me = (z * lax.axis_size("bulk") + x) * lax.axis_size("inner") + c
    pack = 128 // seg
    part = lax.broadcasted_iota(jnp.int32, ids_ref.shape[1:], 1) // seg
    tiles = []
    for j in range(0, ids_ref.shape[0], pack):
        tile = ids_ref[j]
        for q in range(1, pack):
            tile = jnp.where(part == q, ids_ref[j + q], tile)
        tiles.append(tile)
    ids = jnp.concatenate(tiles, axis=1) - me * blocks
    member = jnp.zeros((blocks, lanes), jnp.int32)
    for k in range(ids.shape[0]):
        member = jnp.where(ids[k : k + 1, :] == block, 1, member)
    count = member
    inside = lax.rem(pos, seg)
    shift = 1
    while shift < seg:
        count = count + jnp.where(inside >= shift, pltpu.roll(count, shift, 1), 0)
        shift *= 2
    key = jnp.where(member == 1, (pos // seg) * MOST + count - member, -1)
    key_ref[...] = key
    some = 4 if lanes % (4 * seg) == 0 else lanes // seg
    tall = some * MOST
    width = some * seg
    row = lax.broadcasted_iota(jnp.int32, (tall, width), 0)
    parts = []
    for g in range(lanes // width):
        local = key[:, g * width : (g + 1) * width] - g * tall
        hot = jnp.concatenate(
            [jnp.where(local[b : b + 1, :] == row, 1.0, 0.0) for b in range(blocks)], axis=0
        ).astype(jnp.bfloat16)
        got = jnp.dot(
            hot, x_ref[g * width : (g + 1) * width, :], preferred_element_type=jnp.float32
        )
        parts.append(got.reshape(blocks, 1, tall, got.shape[1]))
    got = jnp.concatenate(parts, axis=1).reshape(blocks, rows, x_ref.shape[1])
    xs_ref[0] = got.astype(jnp.bfloat16)


def columns(rows):
    fill = jnp.zeros((128 - len(rows), 128), jnp.float32)
    turned = jnp.concatenate(list(rows) + [fill], axis=0).T
    return [jnp.broadcast_to(turned[:, b : b + 1], (128, 128)) for b in range(len(rows))]


def half_norms(squares_of):
    lane = lax.broadcasted_iota(jnp.int32, (128, 128), 1)
    wide = jnp.zeros((128, 128), jnp.float32)
    for b, square in enumerate(squares_of):
        wide = jnp.where(lane == b, 0.5 * jnp.sum(square, axis=1, keepdims=True), wide)
    turned = wide.T
    return [turned[b : b + 1, :] for b in range(len(squares_of))]


def squares(fine_ref, b):
    total = jnp.zeros((128, 128), jnp.float32)
    for j in range(0, fine_ref.shape[2], 128):
        wide = fine_ref[b, :, j : j + 128].astype(jnp.float32)
        total = total + wide * wide
    return total


def stats(fine_ref, halves, cws, lives, base, inv_root, key_ref, xs_ref, logit_ref, m_scr, s_scr):
    chunks, per, rows, width = xs_ref.shape
    lanes = key_ref.shape[1] // chunks
    row = lax.broadcasted_iota(jnp.int32, (rows, lanes), 0)
    half_c = [0.5 * jnp.sum(cw * cw, axis=1, keepdims=True) for cw in cws]
    for c in range(chunks):
        prods = [
            lax.dot_general(
                xs_ref[c, b], fine_ref[b], (((1,), (1,)), ((), ())),
                preferred_element_type=jnp.float32,
            )
            for b in range(per)
        ]
        parts = []
        for b in range(per):
            part = jnp.zeros((rows, 128), jnp.float32)
            for j in range(0, width, 128):
                wide = xs_ref[c, b, :, j : j + 128].astype(jnp.float32)
                part = part + wide * cws[b][:, j : j + 128]
            parts.append(part)
        shift = jnp.sum(jnp.concatenate(parts, axis=0), axis=1, keepdims=True)
        logits = []
        for b in range(per):
            add = (shift[b * rows : (b + 1) * rows] - half_c[b]) * inv_root
            logit = (prods[b] - halves[b]) * inv_root + add
            logits.append(jnp.where(lives[b] == 1, logit, -jnp.inf))
        logit = jnp.concatenate(logits, axis=0)
        m = jnp.max(logit, axis=1, keepdims=True)
        s = jnp.sum(jnp.exp(logit - m), axis=1, keepdims=True)
        logit_ref[c] = logit.reshape(per, rows, 128)
        part = pl.ds(c * lanes, lanes)
        tops, sums = [], []
        for b in range(per):
            hot = key_ref[pl.ds(base + b, 1), part] == row
            at = slice(b * rows, (b + 1) * rows)
            tops.append(jnp.sum(jnp.where(hot, m[at], 0.0), axis=0, keepdims=True))
            sums.append(jnp.sum(jnp.where(hot, s[at], 0.0), axis=0, keepdims=True))
        for b in range(per):
            m_scr[pl.ds(base + b, 1), part] = tops[b]
            s_scr[pl.ds(base + b, 1), part] = sums[b]


def finish(key_ref, m_scr, s_scr, stat_ref):
    has = key_ref[...] >= 0
    large = jnp.where(has, m_scr[...], LOW)
    top = jnp.max(large, axis=0, keepdims=True)
    term = s_scr[...] * jnp.exp(large - top)
    stat_ref[0:1, :] = top
    stat_ref[1:2, :] = jnp.sum(jnp.where(has, term, 0.0), axis=0, keepdims=True)


def refresh(fine_ref, new_ref, lives, base, key_ref, xs_ref, logit_ref, point_ref, norms):
    chunks, per, rows, width = xs_ref.shape
    lanes = key_ref.shape[1] // chunks
    row = lax.broadcasted_iota(jnp.int32, (rows, lanes), 0)
    mass = [jnp.full((1, 128), PRIOR, jnp.float32) for _ in range(per)]
    weights = []
    for c in range(chunks):
        part = pl.ds(c * lanes, lanes)
        tops, invs = [], []
        for b in range(per):
            hot = key_ref[pl.ds(base + b, 1), part] == row
            both = []
            for k in range(2):
                picked = jnp.where(hot, point_ref[k : k + 1, part], 0.0)
                both.append(jnp.sum(picked, axis=1, keepdims=True))
            tops.append(both[0])
            invs.append(both[1])
        inv = jnp.concatenate(invs, axis=0)
        top = jnp.where(inv > 0.0, jnp.concatenate(tops, axis=0), -LOW)
        logit = logit_ref[c].reshape(per * rows, 128)
        wide = (jnp.exp(logit - top) * inv).astype(jnp.bfloat16).astype(jnp.float32)
        turned = wide.T.astype(jnp.bfloat16)
        weights.append([turned[:, b * rows : (b + 1) * rows] for b in range(per)])
        for b in range(per):
            at = slice(b * rows, (b + 1) * rows)
            mass[b] = mass[b] + jnp.sum(wide[at], axis=0, keepdims=True)
    live_mass = [jnp.where(lives[b] == 1, mass[b], 0.0) for b in range(per)]
    both = columns([1.0 / m for m in mass] + live_mass)
    recips, shares = both[:per], both[per:]
    squares_of, coarse = [], []
    for b in range(per):
        square = jnp.zeros((128, 128), jnp.float32)
        sums = []
        for j in range(0, width, 256):
            size = min(256, width - j)
            total = jnp.zeros((128, size), jnp.float32)
            for c in range(chunks):
                total = total + jnp.dot(
                    weights[c][b], xs_ref[c, b, :, j : j + size],
                    preferred_element_type=jnp.float32,
                )
            for k in range(0, size, 128):
                at = slice(j + k, j + k + 128)
                whole = PRIOR * fine_ref[b, :, at].astype(jnp.float32) + total[:, k : k + 128]
                new = (whole * recips[b]).astype(jnp.bfloat16)
                new_ref[b, :, at] = new
                new = new.astype(jnp.float32)
                sums.append(jnp.sum(new * shares[b], axis=0, keepdims=True))
                if norms:
                    square = square + new * new
        squares_of.append(square)
        out = jnp.concatenate(sums, axis=1) / jnp.sum(live_mass[b], axis=1, keepdims=True)
        coarse.append(out.astype(jnp.bfloat16).astype(jnp.float32))
    return coarse, half_norms(squares_of) if norms else None


def rows_of(ref, base, per):
    return [ref[pl.ds(base + b, 1), :] for b in range(per)]


def first_kernel(inv_root, fine_ref, coarse_ref, live_ref, key_ref, xs_ref, logit_ref, stat_ref,
                 m_scr, s_scr, coarse_scr):
    i = pl.program_id(0)
    per = fine_ref.shape[0]
    base = i * per

    @pl.when(i == 0)
    def _():
        coarse_scr[...] = coarse_ref[...].astype(jnp.float32)

    halves = half_norms([squares(fine_ref, b) for b in range(per)])
    stats(fine_ref, halves, rows_of(coarse_scr, base, per), rows_of(live_ref, base, per), base,
          inv_root, key_ref, xs_ref, logit_ref, m_scr, s_scr)

    @pl.when(i == pl.num_programs(0) - 1)
    def _():
        finish(key_ref, m_scr, s_scr, stat_ref)


def middle_kernel(inv_root, fine_ref, live_ref, key_ref, xs_ref, logit_ref, point_ref,
                  new_ref, out_logit_ref, stat_ref, m_scr, s_scr):
    i = pl.program_id(0)
    per = fine_ref.shape[0]
    base = i * per
    lives = rows_of(live_ref, base, per)
    coarse, halves = refresh(
        fine_ref, new_ref, lives, base, key_ref, xs_ref, logit_ref, point_ref, True
    )
    stats(new_ref, halves, coarse, lives, base, inv_root, key_ref, xs_ref, out_logit_ref, m_scr,
          s_scr)

    @pl.when(i == pl.num_programs(0) - 1)
    def _():
        finish(key_ref, m_scr, s_scr, stat_ref)


def last_kernel(fine_ref, live_ref, key_ref, xs_ref, logit_ref, point_ref, new_ref, coarse_ref,
                coarse_scr):
    i = pl.program_id(0)
    per = fine_ref.shape[0]
    base = i * per
    coarse, _ = refresh(
        fine_ref, new_ref, rows_of(live_ref, base, per), base, key_ref, xs_ref, logit_ref,
        point_ref, False
    )
    for b in range(per):
        coarse_scr[pl.ds(base + b, 1), :] = coarse[b]

    @pl.when(i == pl.num_programs(0) - 1)
    def _():
        coarse_ref[...] = coarse_scr[...].astype(jnp.bfloat16)


MESH = pl.DeviceIdType.MESH


def place():
    _, width, cores = [lax.axis_size(a) for a in AXES]
    group = lax.axis_index("groups")
    z, x, c = [lax.axis_index(a) for a in AXES]

    def device(n):
        return (group, n // (width * cores), lax.rem(n // cores, width), lax.rem(n, cores))

    return (z * width + x) * cores + c, device


def greet(owners, me, device):
    barrier = pltpu.get_barrier_semaphore()

    def hello(d, carry):
        peer = lax.rem(me + d, owners)
        pl.semaphore_signal(barrier, inc=1, device_id=device(peer), device_id_type=MESH)
        return carry

    lax.fori_loop(1, owners, hello, 0)
    pl.semaphore_wait(barrier, owners - 1)


def direct(owners, me, device, src, dst, send_sem, recv_sem):
    def copy(peer, slot):
        return pltpu.make_async_remote_copy(
            src_ref=src, dst_ref=dst.at[slot], send_sem=send_sem.at[peer],
            recv_sem=recv_sem.at[slot], device_id=device(peer), device_id_type=MESH,
        )

    def start(d, carry):
        copy(lax.rem(me + d, owners), me).start()
        return carry

    def wait(d, carry):
        peer = lax.rem(me + d, owners)
        copy(peer, peer).wait_recv()
        copy(peer, me).wait_send()
        return carry

    return (lambda: lax.fori_loop(1, owners, start, 0)), (
        lambda: lax.fori_loop(1, owners, wait, 0)
    )


def exchange_kernel(owners, src_ref, point_ref, dst_ref, send_sem, recv_sem, own_sem):
    me, device = place()
    own = pltpu.make_async_copy(src_ref, dst_ref.at[me], own_sem)
    own.start()
    greet(owners, me, device)
    start, wait = direct(owners, me, device, src_ref, dst_ref, send_sem, recv_sem)
    start()
    own.wait()
    wait()
    top = dst_ref[0, 0:1, :]
    for n in range(1, owners):
        top = jnp.maximum(top, dst_ref[n, 0:1, :])
    total = jnp.zeros_like(top)
    for n in range(owners):
        total = total + dst_ref[n, 1:2, :] * jnp.exp(dst_ref[n, 0:1, :] - top)
    point_ref[0:1, :] = top
    point_ref[1:2, :] = 1.0 / total


def spread_stats(stat):
    owners = lax.axis_size(AXES)
    return pl.pallas_call(
        functools.partial(exchange_kernel, owners),
        in_specs=[pl.BlockSpec(memory_space=pltpu.VMEM)],
        out_specs=pl.BlockSpec(memory_space=pltpu.VMEM),
        out_shape=jax.ShapeDtypeStruct(stat.shape, stat.dtype),
        scratch_shapes=[
            pltpu.VMEM((owners,) + stat.shape, stat.dtype),
            pltpu.SemaphoreType.DMA((owners,)),
            pltpu.SemaphoreType.DMA((owners,)),
            pltpu.SemaphoreType.DMA,
        ],
        compiler_params=pltpu.CompilerParams(
            collective_id=1, has_side_effects=True, vmem_limit_bytes=VMEM
        ),
        name="exchange",
    )(stat)


def gather_kernel(x_ref, ids_ref, out_ref, ids_out_ref, z_send, x_send, c_send, recv, ids_send,
                  ids_recv, own_sem):
    depth, width, cores = [lax.axis_size(a) for a in AXES]
    owners = depth * width * cores
    group = lax.axis_index("groups")
    z, x, c = [lax.axis_index(a) for a in AXES]
    me, device = place()

    def slot_of(zz, xx, cc):
        return (zz * width + xx) * cores + cc

    own = pltpu.make_async_copy(x_ref, out_ref.at[me], own_sem.at[0])
    own.start()
    own_ids = pltpu.make_async_copy(ids_ref, ids_out_ref.at[me], own_sem.at[1])
    own_ids.start()
    greet(owners, me, device)

    count = recv.shape[0]
    tall = x_ref.shape[0] // count

    def part(ref, h):
        return ref.at[pl.ds(h * tall, tall)]

    def copy(src, slot, sem, h, target):
        return pltpu.make_async_remote_copy(
            src_ref=part(src, h), dst_ref=part(out_ref.at[slot], h), send_sem=sem,
            recv_sem=recv.at[h, slot], device_id=target, device_id_type=MESH,
        )

    def arrive(slot, h):
        copy(x_ref, slot, own_sem.at[0], h, (group, z, x, c)).wait_recv()

    def along_z(src, zz, step, h):
        side = 0 if step > 0 else 1
        return copy(src, slot_of(zz, x, c), z_send.at[h, side, zz], h, (group, z + step, x, c))

    def along_x(src, zz, e, h):
        return copy(
            src, slot_of(zz, x, c), x_send.at[h, e, zz], h, (group, z, lax.rem(x + e, width), c)
        )

    def along_c(src, zz, xx, e, h):
        return copy(
            src, slot_of(zz, xx, c), c_send.at[h, e, zz * width + xx], h,
            (group, z, x, lax.rem(c + e, cores)),
        )

    def spread(src, zz, h):
        for e in range(1, width):
            along_x(src, zz, e, h).start()
        for e in range(1, cores):
            along_c(src, zz, x, e, h).start()

    def from_x(zz):
        for e in range(1, width):
            xx = lax.rem(x + e, width)
            slot = slot_of(zz, xx, c)
            for h in range(count):
                arrive(slot, h)
                for f in range(1, cores):
                    along_c(out_ref.at[slot], zz, xx, f, h).start()

    for h in range(count):
        @pl.when(z + 1 < depth)
        def _():
            along_z(x_ref, z, 1, h).start()

        @pl.when(z > 0)
        def _():
            along_z(x_ref, z, -1, h).start()

        spread(x_ref, z, h)

    start_ids, wait_ids = direct(owners, me, device, ids_ref, ids_out_ref, ids_send, ids_recv)
    start_ids()

    def step(t, carry):
        for h in range(count):
            for sign in (1, -1):
                zz = z - sign * t
                known = (zz >= 0) & (zz < depth)
                onward = (z + sign >= 0) & (z + sign < depth)

                @pl.when(known)
                def _():
                    slot = slot_of(zz, x, c)
                    arrive(slot, h)

                    @pl.when(onward)
                    def _():
                        along_z(out_ref.at[slot], zz, sign, h).start()

                    spread(out_ref.at[slot], zz, h)

        for sign in (1, -1):
            zz = z - sign * (t - 1)

            @pl.when((zz >= 0) & (zz < depth) & ((t > 1) | (sign == 1)))
            def _():
                from_x(zz)

        return carry

    lax.fori_loop(1, depth, step, 0)
    for sign in (1, -1):
        zz = z - sign * (depth - 1)

        @pl.when((zz >= 0) & (zz < depth))
        def _():
            from_x(zz)

    def last(zz, carry):
        for h in range(count):
            for e in range(1, cores):
                for xx in range(width):
                    arrive(slot_of(zz, xx, lax.rem(c + e, cores)), h)
        return carry

    lax.fori_loop(0, depth, last, 0)
    wait_ids()

    def sent(zz, carry):
        for h in range(count):
            @pl.when((zz <= z) & (z + 1 < depth))
            def _():
                along_z(x_ref, zz, 1, h).wait_send()

            @pl.when((zz >= z) & (z > 0))
            def _():
                along_z(x_ref, zz, -1, h).wait_send()

            for e in range(1, width):
                along_x(x_ref, zz, e, h).wait_send()
            for e in range(1, cores):
                for xx in range(width):
                    along_c(x_ref, zz, xx, e, h).wait_send()
        return carry

    lax.fori_loop(0, depth, sent, 0)
    own.wait()
    own_ids.wait()


def spread_points(points, ids):
    depth, width, cores = [lax.axis_size(a) for a in AXES]
    owners = depth * width * cores
    return pl.pallas_call(
        gather_kernel,
        in_specs=[pl.BlockSpec(memory_space=pl.ANY)] * 2,
        out_specs=[pl.BlockSpec(memory_space=pl.ANY)] * 2,
        out_shape=[
            jax.ShapeDtypeStruct((owners,) + points.shape, points.dtype),
            jax.ShapeDtypeStruct((owners,) + ids.shape, ids.dtype),
        ],
        scratch_shapes=[
            pltpu.SemaphoreType.DMA((HALVES, 2, depth)),
            pltpu.SemaphoreType.DMA((HALVES, width, depth)),
            pltpu.SemaphoreType.DMA((HALVES, cores, depth * width)),
            pltpu.SemaphoreType.DMA((HALVES, owners)),
            pltpu.SemaphoreType.DMA((owners,)),
            pltpu.SemaphoreType.DMA((owners,)),
            pltpu.SemaphoreType.DMA((2,)),
        ],
        compiler_params=pltpu.CompilerParams(collective_id=0, has_side_effects=True),
        name="gather",
    )(points, ids)


def shards(points, coarse_ids, fine_cent, slot_live, coarse_cent):
    seg, top_count = coarse_ids.shape
    blocks, slots, feature = fine_cent.shape
    owners = lax.axis_size(AXES)
    total = owners * seg
    senders = min(owners, 16)
    chunks = owners // senders
    lanes = senders * seg
    rows = senders * MOST
    inv_root = 1.0 / math.sqrt(feature)
    per = min(blocks, PER)
    steps = blocks // per
    f32, bf16 = jnp.float32, jnp.bfloat16
    params = pltpu.CompilerParams(vmem_limit_bytes=VMEM, dimension_semantics=("arbitrary",))

    ids = jnp.concatenate([coarse_ids.T] * (128 // seg), axis=1)
    all_points, all_ids = spread_points(points, ids)
    all_points = all_points.reshape(total, feature)

    key, xs = pl.pallas_call(
        functools.partial(pick_kernel, seg),
        grid=(chunks,),
        in_specs=[
            pl.BlockSpec((senders, top_count, 128), lambda i: (i, 0, 0)),
            pl.BlockSpec((lanes, feature), lambda i: (i, 0)),
        ],
        out_specs=[
            pl.BlockSpec((blocks, lanes), lambda i: (0, i)),
            pl.BlockSpec((1, blocks, rows, feature), lambda i: (i, 0, 0, 0)),
        ],
        out_shape=[
            jax.ShapeDtypeStruct((blocks, total), jnp.int32),
            jax.ShapeDtypeStruct((chunks, blocks, rows, feature), bf16),
        ],
        compiler_params=params,
        name="pick",
    )(all_ids, all_points)

    fine_spec = pl.BlockSpec((per, slots, feature), lambda i: (i, 0, 0))
    coarse_spec = pl.BlockSpec((blocks, feature), lambda i: (0, 0))
    live_spec = pl.BlockSpec((blocks, slots), lambda i: (0, 0))
    key_spec = pl.BlockSpec((blocks, total), lambda i: (0, 0))
    xs_spec = pl.BlockSpec((chunks, per, rows, feature), lambda i: (0, i, 0, 0))
    logit_spec = pl.BlockSpec((chunks, per, rows, slots), lambda i: (0, i, 0, 0))
    stat_spec = pl.BlockSpec((2, total), lambda i: (0, 0))
    fine_shape = jax.ShapeDtypeStruct((blocks, slots, feature), bf16)
    logit_shape = jax.ShapeDtypeStruct((chunks, blocks, rows, slots), f32)
    stat_shape = jax.ShapeDtypeStruct((2, total), f32)
    grid_scr = pltpu.VMEM((blocks, total), f32)
    coarse_scr = pltpu.VMEM((blocks, feature), f32)

    logit, stat = pl.pallas_call(
        functools.partial(first_kernel, inv_root),
        grid=(steps,),
        in_specs=[fine_spec, coarse_spec, live_spec, key_spec, xs_spec],
        out_specs=[logit_spec, stat_spec],
        out_shape=[logit_shape, stat_shape],
        scratch_shapes=[grid_scr, grid_scr, coarse_scr],
        compiler_params=params,
        name="first",
    )(fine_cent, coarse_cent, slot_live, key, xs)
    fine = fine_cent
    for _ in range(ITERS - 1):
        every = spread_stats(stat)
        fine, logit, stat = pl.pallas_call(
            functools.partial(middle_kernel, inv_root),
            grid=(steps,),
            in_specs=[fine_spec, live_spec, key_spec, xs_spec, logit_spec, stat_spec],
            out_specs=[fine_spec, logit_spec, stat_spec],
            out_shape=[fine_shape, logit_shape, stat_shape],
            scratch_shapes=[grid_scr, grid_scr],
            compiler_params=params,
            name="middle",
        )(fine, slot_live, key, xs, logit, every)
    every = spread_stats(stat)
    fine, coarse = pl.pallas_call(
        last_kernel,
        grid=(steps,),
        in_specs=[fine_spec, live_spec, key_spec, xs_spec, logit_spec, stat_spec],
        out_specs=[fine_spec, coarse_spec],
        out_shape=[fine_shape, jax.ShapeDtypeStruct((blocks, feature), bf16)],
        scratch_shapes=[coarse_scr],
        compiler_params=params,
        name="last",
    )(fine, slot_live, key, xs, logit, every)
    return fine, coarse


def solution(mesh):
    spec = P(("groups",) + AXES)
    return jax.shard_map(
        shards, mesh=mesh, in_specs=(spec,) * 5, out_specs=(spec,) * 2, check_vma=False
    )
```

time: 93.3 us -> 89.3 us (0.957)
  Pallas kernels: 90.5 us -> 86.8 us
    pallas_call x1, Pallas kernels: 6.47 us -> 4.62 us  [shards(): pl.pallas_call(functools.partial(pick_kernel, seg), grid=(chunks,), in_sp...]
    pallas_call x1, Pallas kernels: 26.5 us -> 24.7 us  [spread_points(): pl.pallas_call(gather_kernel, in_specs=[pl.BlockSpec(memory_space=pl.ANY)...]
    pallas_call x1, Pallas kernels: 10.5 us -> 8.9 us  [shards(): pl.pallas_call(functools.partial(first_kernel, inv_root), grid=(steps,),...]
    pallas_call x2, Pallas kernels: 16.3 us -> 17.6 us  [spread_stats(): pl.pallas_call(functools.partial(exchange_kernel, owners), in_specs=[pl.B...]
where the time goes in v3:
time: 89.3 us; the launch traced here: 88.8 us
  Pallas kernels  86.8 us (97%)
  other arithmetic  1.43 us (2%)
    pallas_call x1, Pallas kernels, spread_points(): pl.pallas_call(gather_kernel, in_specs=[pl.BlockSpec(memory_space=pl.ANY)...  24.7 us
    pallas_call x1, Pallas kernels, shards(): pl.pallas_call(functools.partial(middle_kernel, inv_root), grid=(steps,),...  18.1 us
    pallas_call x2, Pallas kernels, spread_stats(): pl.pallas_call(functools.partial(exchange_kernel, owners), in_specs=[pl.B...  17.6 us
    pallas_call x1, Pallas kernels, shards(): pl.pallas_call(last_kernel, grid=(steps,), in_specs=[fine_spec, live_spec...  12.8 us
    pallas_call x1, Pallas kernels, shards(): pl.pallas_call(functools.partial(first_kernel, inv_root), grid=(steps,),...  8.9 us
    pallas_call x1, Pallas kernels, shards(): pl.pallas_call(functools.partial(pick_kernel, seg), grid=(chunks,), in_sp...  4.62 us

profile of v3, /device:TPU:0, one launch (start us, length us, event | category | flops | bytes accessed | tf_op | source)
XLA Modules:
  0.0 88.8 jit_solution(6311917053312056268)
XLA Ops:
  0.6 1.4 %pad_add_fusion.ids_ref = s32[8,128]{1,0:T(8,128)} fusion(s32[8,64]{1,0:T(8,128)} %bitcast.3), kind=kLoop, calls=%fused_computation | loop fusion | flops 1024 | bytes 6144 | tf_op jit(solution)/shard_map/concatenate | solution.py:523
  2.1 24.7 %gather.1 = (bf16[16,64,1152]{2,1,0:T(8,128)(2,1)}, s32[16,8,128]{2,1,0:T(8,128)}) custom-call(bf16[64,1152]{1,0:T(8,128)(2,1)} %x_ref.1, s32[8,128]{1,0:T(8,128)} %pad_add_fusion.ids_ref), custom_call_target="tpu_custom_call" | custom-call | tf_op jit(solution)/shard_map/gather/pallas_call | solution.py:486
  26.8 4.6 %pick.1 = (s32[32,1024]{1,0:T(8,128)}, bf16[1,32,32,1152]{3,2,1,0:T(8,128)(2,1)}) custom-call(s32[16,8,128]{2,1,0:T(8,128)} %get-tuple-element.11.ids_ref, bf16[1024,1152]{1,0:T(8,128)(2,1)} %bitcast.2), custom_call_target="tpu_custom_call" | custom-call | tf_op jit(solution)/shard_map/pick/pallas_call | solution.py:527
  31.4 8.9 %first.1 = (f32[1,32,32,128]{3,2,1,0:T(8,128)}, f32[2,1024]{1,0:T(2,128)}) custom-call(bf16[32,128,1152]{2,1,0:T(8,128)(2,1)} %fine_ref.3, bf16[32,1152]{1,0:T(8,128)(2,1)} %coarse_ref.1, s32[32,128]{1,0:T(8,128)} %live_ref.5, s32[32,1024]{1,0:T(8,128)} %get-tuple-element.13.key_ref, bf16[1,32,32,1152]{3,2,1,0:T(8,128)(2,1)} %get-tuple-element.14.xs_ref), custom_call_target="tpu_custom_call" | custom-call | tf_op jit(solution)/shard_map/first/pallas_call | solution.py:559
  40.3 8.3 %exchange.2.point_ref = f32[2,1024]{1,0:T(2,128)} custom-call(f32[2,1024]{1,0:T(2,128)} %get-tuple-element.16.src_ref), custom_call_target="tpu_custom_call" | custom-call | tf_op jit(solution)/shard_map/exchange/pallas_call | solution.py:322
  48.6 18.1 %middle.1 = (bf16[32,128,1152]{2,1,0:T(8,128)(2,1)}, f32[1,32,32,128]{3,2,1,0:T(8,128)}, f32[2,1024]{1,0:T(2,128)}) custom-call(bf16[32,128,1152]{2,1,0:T(8,128)(2,1)} %fine_ref.3, s32[32,128]{1,0:T(8,128)} %live_ref.5, s32[32,1024]{1,0:T(8,128)} %get-tuple-element.13.key_ref, bf16[1,32,32,1152]{3,2,1,0:T(8,128)(2,1)} %get-tuple-element.14.xs_ref, ...), custom_call_target="tpu_custom_call" | custom-call | tf_op jit(solution)/shard_map/middle/pallas_call | solution.py:572
  66.7 9.3 %exchange.3.point_ref = f32[2,1024]{1,0:T(2,128)} custom-call(f32[2,1024]{1,0:T(2,128)} %get-tuple-element.19.src_ref), custom_call_target="tpu_custom_call" | custom-call | tf_op jit(solution)/shard_map/exchange/pallas_call | solution.py:322
  76.0 12.8 %last.1 = (bf16[32,128,1152]{2,1,0:T(8,128)(2,1)}, bf16[32,1152]{1,0:T(8,128)(2,1)}) custom-call(bf16[32,128,1152]{2,1,0:T(8,128)(2,1)} %get-tuple-element.17.fine_ref, s32[32,128]{1,0:T(8,128)} %live_ref.5, s32[32,1024]{1,0:T(8,128)} %get-tuple-element.13.key_ref, bf16[1,32,32,1152]{3,2,1,0:T(8,128)(2,1)} %get-tuple-element.14.xs_ref, ...), custom_call_target="tpu_custom_call" | custom-call | tf_op jit(solution)/shard_map/last/pallas_call | solution.py:583
